TPU v7x, 512 devices: a whole 4x8x8 slice. The times are simulated.
512 devices in a mesh: node: 32 (over x, y), chan: 16 (over z, core).
Axes of the slice: x: 4, y: 8, z: 8, core: 2. Of those that a mesh axis runs over, the one named last changes fastest.
Arguments:
- features: bfloat16 [57344, 1024], P('node', 'chan'), may hold values from -0.046875 to 0.046875
- weight: bfloat16 [1024, 1024], P('node', 'chan'), may hold values from -0.375 to 0.375
- pre_clean: bfloat16 [57344, 1024], P('node', 'chan'), may hold values from -6 to 6
- pre_corrupt: bfloat16 [57344, 1024], P('node', 'chan'), may hold values from -6 to 6
- grad_clean: bfloat16 [57344, 1024], P('node', 'chan'), may hold values from -6 to 6
- grad_corrupt: bfloat16 [57344, 1024], P('node', 'chan'), may hold values from -6 to 6
- slopes: float32 [1024], P('chan'), may hold values from 0.05 to 0.5
- adj_vals: bfloat16 [448, 5, 128, 128], P('node'), may hold values from 0 to 0.07861328
- adj_cols: int32 [448, 5], P('node'), may hold values from 0 to 447, as said below
- adj_count: int32 [448], P('node'), may hold values from 1 to 5, as said below
- shuffle_from: int32 [448], replicated, may hold values from 0 to 447, as said below
Outputs:
- grad_weight: float32 [1024, 1024], P('node', 'chan')
- grad_features: bfloat16 [57344, 1024], P('node', 'chan')
Inputs may be any that keep to these rules, and one draw needn't show every extreme that they name: `adj_cols`: entry [b, k] is a block within 2 of b, and entry [b, 0] is b itself. Slots k < adj_count[b] of row block b hold edge tiles; the other slots are padding and are not read. `shuffle_from`: A permutation of the blocks. The 14 blocks of one index of node take their rows from exactly 14 distinct indices of node, 1 block from each; among these are the index just after it and the index 16 away, counted round.
All inputs are finite; a program needn't handle non-finite values.
Results may differ from a plain program's by a relative error of at most 0.023.
Values may be sent and summed in bfloat16 or wider, within the bound.
A program may use at most 64 MiB of HBM per device.

v0:
```python
import jax
import jax.numpy as jnp
from jax import lax
from jax.sharding import PartitionSpec as P


def shifted(value, axis, by):
    size = lax.axis_size(axis)
    pairs = [(i, i + by) for i in range(size) if 0 <= i + by < size]
    return lax.ppermute(value, axis, pairs)


def local_grad(grad_part, pre_part, slopes):
    factor = jnp.where(pre_part > 0, 1.0, slopes[None, :])
    return (grad_part.astype(jnp.float32) * factor).astype(jnp.bfloat16)


def local(
    features,
    weight,
    pre_clean,
    pre_corrupt,
    grad_clean,
    grad_corrupt,
    slopes,
    adj_vals,
    adj_cols,
    adj_count,
    shuffle_from,
):
    row_count, chan_width = features.shape
    blocks = adj_vals.shape[0]
    tile_slots = adj_vals.shape[1]
    tile_rows = adj_vals.shape[2]
    band_reach = (tile_slots - 1) // 2
    my_index = lax.axis_index("node")
    dev_count = lax.axis_size("node")
    d_clean = local_grad(grad_clean, pre_clean, slopes)
    d_corrupt = local_grad(grad_corrupt, pre_corrupt, slopes)
    stacked = jnp.concatenate([d_clean, d_corrupt], axis=1).reshape(
        blocks, tile_rows, 2 * chan_width
    )
    contrib = jnp.einsum("bkpq,bpc->bkqc", adj_vals, stacked, preferred_element_type=jnp.float32)
    span_blocks = blocks + 2 * band_reach
    targets = adj_cols - (my_index * blocks - band_reach)
    live_mask = jnp.arange(tile_slots)[None, :] < adj_count[:, None]
    chooser = (
        (targets.reshape(-1)[None, :] == jnp.arange(span_blocks)[:, None])
        & live_mask.reshape(-1)[None, :]
    ).astype(jnp.float32)
    summed = jnp.dot(
        chooser, contrib.reshape(blocks * tile_slots, -1), precision=lax.Precision.HIGHEST
    )
    summed = summed.reshape(span_blocks, tile_rows, 2 * chan_width)
    from_prev = shifted(summed[band_reach + blocks :].astype(jnp.bfloat16), "node", 1).astype(
        jnp.float32
    )
    from_next = shifted(summed[:band_reach].astype(jnp.bfloat16), "node", -1).astype(jnp.float32)
    remaining = blocks - band_reach
    middle = summed[band_reach : band_reach + blocks]
    middle = (
        middle
        + jnp.pad(from_prev, ((0, remaining), (0, 0), (0, 0)))
        + jnp.pad(from_next, ((remaining, 0), (0, 0), (0, 0)))
    )
    backprop = middle.astype(jnp.bfloat16).reshape(row_count, 2 * chan_width)
    back_clean = backprop[:, :chan_width]
    back_corrupt = backprop[:, chan_width:]
    my_blocks = my_index * blocks + jnp.arange(blocks)
    all_blocks = jnp.arange(shuffle_from.shape[0])
    one_hot = (shuffle_from[None, :] == my_blocks[:, None]).astype(jnp.int32)
    source_block = jnp.sum(one_hot * all_blocks[None, :], axis=1)
    wanted = (source_block[:, None] * tile_rows + jnp.arange(tile_rows)[None, :]).reshape(-1)
    portion = lax.all_gather(back_corrupt, "node", axis=0, tiled=True)
    inside = (wanted >= 0) & (wanted < portion.shape[0])
    fetched = jnp.take(portion, jnp.clip(wanted, 0, portion.shape[0] - 1), axis=0)
    unshuffled = jnp.where(inside[:, None], fetched, jnp.zeros_like(back_corrupt))
    combined = jnp.concatenate([back_clean, unshuffled], axis=1)
    product = lax.dot_general(
        lax.all_gather(features, "chan", axis=1, tiled=True),
        combined,
        (((0,), (0,)), ((), ())),
        preferred_element_type=jnp.float32,
    )
    partial_w = product[:, :chan_width] + product[:, chan_width:]
    share_rows = partial_w.shape[0] // dev_count
    summed_w = lax.psum(partial_w.astype(jnp.bfloat16), "node").astype(jnp.float32)
    grad_weight = lax.dynamic_slice_in_dim(summed_w, my_index * share_rows, share_rows, 0)
    portion = lax.all_gather(weight, "node", axis=0, tiled=True)
    doubled = jnp.concatenate([portion, portion], axis=1)
    partial_x = lax.dot_general(
        combined, doubled, (((1,), (1,)), ((), ())), preferred_element_type=jnp.float32
    )
    grad_features = lax.psum_scatter(
        partial_x.astype(jnp.bfloat16), "chan", scatter_dimension=1, tiled=True
    )
    return (grad_weight, grad_features)


def solution(mesh):
    placed = (
        P("node", "chan"),
        P("node", "chan"),
        P("node", "chan"),
        P("node", "chan"),
        P("node", "chan"),
        P("node", "chan"),
        P("chan"),
        P("node", None, None, None),
        P("node", None),
        P("node"),
        P(),
    )
    return jax.shard_map(
        local,
        mesh=mesh,
        in_specs=placed,
        out_specs=(P("node", "chan"), P("node", "chan")),
        check_vma=False,
    )
```

profile of v0, /device:TPU:6, one launch (start us, length us, event | category | flops | bytes accessed | tf_op | source)
XLA Modules:
  0.0 460.4 jit_solution(3532302501971480463)
XLA Ops:
  7.2 1.4 copy.28
  8.6 1.2 copy.29
  9.8 1.9 copy.30
  11.7 1.9 copy.31
  13.6 1.5 multiply_convert_fusion.1
  15.4 2.9 convolution_bitcast_fusion
  18.3 5.7 %copy.33 = f32[14,5,128,128]{3,2,1,0:T(8,128)} copy(f32[14,5,128,128]{2,3,1,0:T(8,128)} %convolution_bitcast_fusion) | data formatting | bytes 9175040 | tf_op jit(solution)/shard_map/bkpq,bpc->bkqc/dot_general | solution.py:43
  24.1 2.9 pad.25
  27.0 4.9 %copy.38 = f32[9,8,128,128]{3,1,2,0:T(8,128)} copy(f32[9,8,128,128]{3,2,1,0:T(8,128)S(1)} %bitcast.49) | data formatting | bytes 9437184
  32.3 4.1 fusion.24
  36.5 3.5 collective-permute-start
  40.0 4.5 collective-permute-start.1
  44.8 1.5 collective-permute-done.1
  46.4 1.0 fusion.23
  48.2 49.9 %all_gather.11 = bf16[1024,64]{1,0:T(8,128)(2,1)S(1)} all-gather(bf16[32,64]{1,0:T(8,128)(2,1)S(1)} %copy-done.1), channel_id=1, replica_groups=mesh['node'=32,'chan'=16] {'node'}, dimensions={0}, use_global_device_ids=true | all-gather | bytes 135168 | tf_op jit(solution)/shard_map/all_gather | solution.py:89
  98.6 86.6 %all-gather.3.cloned.1.call-done = bf16[57344,64]{1,0:T(8,128)(2,1)} async-done(((bf16[1792,64]{1,0:T(8,128)(2,1)}), bf16[57344,64]{1,0:T(8,128)(2,1)}) %all-gather.3.cloned.1.call-update) | async-done | bytes 7340048 | tf_op jit(solution)/shard_map/all_gather | solution.py:74
  185.2 11.3 %gather_fusion = bf16[1792,64]{1,0:T(8,128)(2,1)} fusion(bf16[57344,64]{1,0:T(8,128)(2,1)} %all-gather.3.cloned.1.call-done, s32[2048]{0:T(1024)S(1)} %pad_clamp_fusion), kind=kCustom, calls=%fused_computation | custom fusion | bytes 465920 | tf_op jit(solution)/shard_map/jit(_take)/gather | solution.py:76
  196.5 2.7 select_select_fusion
  199.2 32.5 %all-gather.5.cloned.1.call-done = bf16[1792,1024]{0,1:T(8,128)(2,1)} async-done(((bf16[1792,64]{0,1:T(8,128)(2,1)}), bf16[1792,1024]{0,1:T(8,128)(2,1)}) %all-gather.5.cloned.1.call-update) | async-done | bytes 3670032 | tf_op jit(solution)/shard_map/all_gather | solution.py:80
  231.7 3.7 convolution_bitcast_fusion.1
  236.1 3.0 convolution_convert_fusion
  239.2 146.7 %all-reduce.4.cloned.1.call-done = bf16[1024,64]{0,1:T(8,128)(2,1)} async-done(((bf16[1024,64]{0,1:T(8,128)(2,1)}), bf16[1024,64]{0,1:T(8,128)(2,1)}) %all-reduce.4.cloned.1.call-update) | async-done | bytes 131088 | tf_op jit(solution)/shard_map/psum | solution.py:87
  385.9 0.8 dynamic-slice_convert_fusion
  387.4 66.4 %reduce-scatter.2.cloned.1.call-done = bf16[1792,64]{0,1:T(8,128)(2,1)} async-done(((bf16[1792,1024]{0,1:T(8,128)(2,1)}), bf16[1792,64]{0,1:T(8,128)(2,1)}) %reduce-scatter.2.cloned.1.call-update) | async-done | bytes 229392 | tf_op jit(solution)/shard_map/reduce_scatter | solution.py:94
  (41 shorter events, 3.8 us)
Async XLA Ops:
  7.2 8.3 %copy-start = (bf16[14,5,128,128]{3,2,1,0:T(8,128)(2,1)S(1)}, bf16[14,5,128,128]{3,2,1,0:T(8,128)(2,1)}, u32[]{:S(2)}) copy-start(bf16[14,5,128,128]{3,2,1,0:T(8,128)(2,1)} %param.18) | copy-start | bytes 6881284
  7.2 178.0 %all-gather.3.cloned.1.call-start = ((), (), s32[]{:S(2)}) async-start(), calls=%async_computation.1 | async-start | bytes 15138816 | tf_op jit(solution)/shard_map/all_gather | solution.py:74
  27.0 4.9 %copy-start.2 = (s32[14,5]{0,1:T(8,128)S(1)}, s32[14,5]{0,1:T(8,128)}, u32[]{:S(2)}) copy-start(s32[14,5]{0,1:T(8,128)} %param.19) | copy-start | bytes 844
  27.0 5.1 %copy-start.4 = (s32[14]{0:T(128)S(1)}, s32[14]{0:T(128)}, u32[]{:S(2)}) copy-start(s32[14]{0:T(128)} %param.20) | copy-start | bytes 172
  36.5 8.3 %collective-permute-start = (bf16[2,128,128]{2,1,0:T(8,128)(2,1)S(1)}, bf16[2,128,128]{2,1,0:T(8,128)(2,1)S(1)}, u32[]{:S(2)}, u32[]{:S(2)}) collective-permute-start(bf16[2,128,128]{2,1,0:T(8,128)(2,1)S(1)} %bitcast.56), channel_id=1, source_target_pairs={{0,16},{16,32},{32,48},{48,64},{64,80},{80,96},{96,112},{112,128},... | collective-permute-start | bytes 196616 | tf_op jit(solution)/shard_map/ppermute | solution.py:10
  40.0 6.4 %collective-permute-start.1 = (bf16[2,128,128]{2,1,0:T(8,128)(2,1)S(1)}, bf16[2,128,128]{2,1,0:T(8,128)(2,1)S(1)}, u32[]{:S(2)}, u32[]{:S(2)}) collective-permute-start(bf16[2,128,128]{2,1,0:T(8,128)(2,1)S(1)} %bitcast.57), channel_id=1, source_target_pairs={{16,0},{32,16},{48,32},{64,48},{80,64},{96,80},{112,96},{128,112},... | collective-permute-start | bytes 196616 | tf_op jit(solution)/shard_map/ppermute | solution.py:10
  44.4 3.8 copy-start.1
  44.6 53.6 %copy-start.3 = (s32[448]{0:T(512)S(1)}, s32[448]{0:T(512)}, u32[]{:S(2)}) copy-start(s32[448]{0:T(512)} %param.21) | copy-start | bytes 5380
  47.4 184.3 %all-gather.5.cloned.1.call-start = ((), (), s32[]{:S(2)}) async-start(), calls=%async_computation.2 | async-start | bytes 3899392 | tf_op jit(solution)/shard_map/all_gather | solution.py:80
  48.1 337.8 %all-reduce.4.cloned.1.call-start = ((), (), s32[]{:S(2)}) async-start(), calls=%async_computation.3 | async-start | bytes 262144 | tf_op jit(solution)/shard_map/psum | solution.py:87
  236.1 217.7 %reduce-scatter.2.cloned.1.call-start = ((), (), s32[]{:S(2)}) async-start(), calls=%async_computation.4 | async-start | bytes 3899392 | tf_op jit(solution)/shard_map/reduce_scatter | solution.py:94
Sparse Core Ops, SparseCore 0:
  47.5 137.6 all-gather.2
  187.3 44.3 all-gather.4
  236.2 149.6 all-reduce.3
  389.5 64.3 reduce-scatter.1
where the time goes:
time: 461 us; the launch traced here: 460 us
  waiting for transfers between devices  335 us (73%)
  blocking collectives  49.9 us (11%)
  local copies, waits for them, and re-layouts  33.5 us (7%)
  between operations  14 us (3%)
  matrix products  13.7 us (3%)
  starting transfers between devices  8.11 us (2%)
  other arithmetic  6.56 us (1%)
    psum x1, waiting for transfers between devices, local(): lax.psum(partial_w.astype(jnp.bfloat16), 'node').astype(jnp.float32)  147 us
    all_gather x1, waiting for transfers between devices, local(): portion = lax.all_gather(back_corrupt, 'node', axis=0, tiled=True)  86.6 us
    reduce_scatter x1, waiting for transfers between devices, local(): lax.psum_scatter(partial_x.astype(jnp.bfloat16), 'chan', scatter_dimensio...  66.4 us
    all_gather x1, blocking collectives, local(): portion = lax.all_gather(weight, 'node', axis=0, tiled=True)  49.9 us
    all_gather x1, waiting for transfers between devices, local(): lax.all_gather(features, 'chan', axis=1, tiled=True)  32.5 us
    unnamed x21, local copies, waits for them, and re-layouts  15.2 us
    gather x1, local copies, waits for them, and re-layouts, local(): jnp.take(portion, jnp.clip(wanted, 0, portion.shape[0] - 1), axis=0)  11.3 us
  transfers between devices with their start and end apart: 6, of which 5 were waited for; matrix products, arithmetic and copies ran while one was open for 4% of the time, Pallas kernels for 0%

commit v1 on v0

v1 whole, which is shorter than its diff:
```python
import functools

import jax
import jax.numpy as jnp
from jax import lax
from jax.experimental import pallas as pl
from jax.experimental.pallas import tpu as pltpu
from jax.sharding import PartitionSpec as P

MESH = pl.DeviceIdType.MESH
BF16 = jnp.bfloat16
F32 = jnp.float32


def band_kernel(
    cols_ref, count_ref, gc_ref, pc_ref, gx_ref, px_ref, slope_ref, adj_ref,
    main_ref, before_ref, after_ref, acc,
):
    blocks, slots, rows, _ = adj_ref.shape
    reach = (slots - 1) // 2
    base = lax.axis_index("node") * blocks - reach
    acc[...] = jnp.zeros_like(acc)
    slope = slope_ref[...]
    spare = blocks + 2 * reach
    for b in range(blocks):
        here = slice(b * rows, (b + 1) * rows)

        def grad(g_ref, p_ref):
            g = g_ref[:, here].astype(F32)
            return jnp.where(p_ref[:, here].astype(F32) > 0, g, g * slope).astype(BF16)

        d = jnp.concatenate([grad(gc_ref, pc_ref), grad(gx_ref, px_ref)], axis=0)
        parts = [jnp.dot(d, adj_ref[b, k], preferred_element_type=F32) for k in range(slots)]
        for k in range(slots):
            target = jnp.where(k < count_ref[b], cols_ref[k, b] - base, spare)
            acc[target] += parts[k]
    main_ref[...] = acc[reach : reach + blocks]
    before_ref[...] = acc[:reach].astype(BF16)
    after_ref[...] = acc[reach + blocks : spare].astype(BF16)


def link_kernel(
    chunks,
    pick_ref, from_ref, main_ref, before_ref, after_ref, feat_ref, wpiece_ref,
    gw_ref, gf_ref,
    gathered, held, corrupt, outgoing, incoming_first, incoming_second, halo, wall, wpair, total, gw_out, gw_in, gw_sum, gw_last,
    halo_send, halo_recv, w_send, w_recv, un_send, un_recv, cw_send, cw_recv, ccw_send, ccw_recv,
    sib_send, sib_recv, gw_send, gw_recv, last_send, last_recv,
):
    nodes = lax.axis_size("node")
    chans = lax.axis_size("chan")
    n = lax.axis_index("node")
    c = lax.axis_index("chan")
    depth = chans // 2
    half = depth // 2
    z = c // 2
    core = lax.rem(c, 2)
    blocks = main_ref.shape[0]
    width = feat_ref.shape[0]
    rows = main_ref.shape[2]
    reach = before_ref.shape[0]
    part = width // chunks
    incoming = (incoming_first, incoming_second)
    right = 2 * lax.rem(z + 1, depth) + core
    left = 2 * lax.rem(z + depth - 1, depth) + core
    sib = 2 * z + 1 - core
    after = lax.rem(n + 1, nodes)
    before = lax.rem(n + nodes - 1, nodes)
    to_n, to_c = 2 * c + n // chans, lax.rem(n, chans)
    fr_n, fr_c = lax.rem(n, 2) * chans + c, n // 2
    to_self = jnp.logical_and(to_n == n, to_c == c)

    def peer(r):
        return lax.rem(n + r, nodes)

    barrier = pltpu.get_barrier_semaphore()

    @pl.loop(1, nodes)
    def _(r):
        pl.semaphore_signal(barrier, inc=1, device_id=(peer(r), c), device_id_type=MESH)

    for who in (right, left, sib):
        pl.semaphore_signal(barrier, inc=1, device_id=(n, who), device_id_type=MESH)

    @pl.when(jnp.logical_not(to_self))
    def _():
        pl.semaphore_signal(barrier, inc=1, device_id=(fr_n, fr_c), device_id_type=MESH)
        pl.semaphore_wait(barrier, nodes + 3)

    @pl.when(to_self)
    def _():
        pl.semaphore_wait(barrier, nodes + 2)

    def halo_copy(src, slot, to):
        return pltpu.make_async_remote_copy(
            src_ref=src, dst_ref=halo.at[slot], send_sem=halo_send.at[slot], recv_sem=halo_recv.at[slot],
            device_id=(to, c), device_id_type=MESH,
        )

    to_after = halo_copy(after_ref, 0, after)
    to_before = halo_copy(before_ref, 1, before)
    to_after.start()
    to_before.start()

    def w_copy(r, slot):
        return pltpu.make_async_remote_copy(
            src_ref=wpiece_ref, dst_ref=wall.at[slot], send_sem=w_send.at[r], recv_sem=w_recv.at[slot],
            device_id=(peer(r), c), device_id_type=MESH,
        )

    to_after.wait_recv()
    to_before.wait_recv()
    for i in range(blocks):
        block = main_ref[i]
        if i < reach:
            block = block + halo[0, i].astype(F32)
        if i >= blocks - reach:
            block = block + halo[1, i - (blocks - reach)].astype(F32)
        held[i] = block[:width]
        corrupt[i] = block[width:].astype(BF16)

    def un_copy(q, r, dest, slot):
        return pltpu.make_async_remote_copy(
            src_ref=outgoing.at[q, dest], dst_ref=incoming[q].at[slot],
            send_sem=un_send.at[q, r], recv_sem=un_recv.at[q, slot],
            device_id=(dest, c), device_id_type=MESH,
        )

    for q in range(chunks):

        @pl.loop(1, nodes)
        def _(r):
            dest = peer(r)
            outgoing[q, dest] = corrupt[pick_ref[dest], q * part : (q + 1) * part]
            un_copy(q, r, dest, n).start()

        incoming[q][n] = corrupt[pick_ref[n], q * part : (q + 1) * part]

    @pl.loop(1, nodes)
    def _(r):
        w_copy(r, n).start()

    wall[n] = wpiece_ref[...]

    def ring_copy(s, q, to_right):
        shard = 2 * lax.rem(z + (depth - s if to_right else s), depth) + core
        where = gathered.at[shard, pl.ds(q * part, part)]
        return pltpu.make_async_remote_copy(
            src_ref=where, dst_ref=where,
            send_sem=(cw_send if to_right else ccw_send).at[s, q],
            recv_sem=(cw_recv if to_right else ccw_recv).at[s, q],
            device_id=(n, right if to_right else left), device_id_type=MESH,
        )

    def sib_copy(t, zz, q):
        where = gathered.at[2 * zz + core, pl.ds(q * part, part)]
        return pltpu.make_async_remote_copy(
            src_ref=where, dst_ref=where, send_sem=sib_send.at[t, q], recv_sem=sib_recv.at[t, q],
            device_id=(n, sib), device_id_type=MESH,
        )

    def goes(s, q, to_right):
        return s + 1 < half or (s + 1 == half and (q < chunks // 2) == to_right)

    def send_on(s, q, to_right):
        if goes(s, q, to_right):
            ring_copy(s, q, to_right).start()

    for q in range(chunks):

        @pl.loop(1, nodes)
        def _(r):
            un_copy(q, r, peer(r), peer(nodes - r)).wait_recv()

        for i in range(blocks):
            gathered[c, q * part : (q + 1) * part, i * rows : (i + 1) * rows] = (
                held[i, q * part : (q + 1) * part] + incoming[q][from_ref[i]].astype(F32)
            ).astype(BF16)
        send_on(0, q, True)
        send_on(0, q, False)
        sib_copy(0, z, q).start()

    @pl.loop(1, nodes)
    def _(r):
        w_copy(r, peer(nodes - r)).wait_recv()

    low = lax.broadcasted_iota(jnp.int32, wpiece_ref.shape, 1) < width

    def swap(value):
        return pltpu.roll(value, width, 1)

    short = wpiece_ref.shape[0]
    for zz in range(depth):
        for h in range(2):
            one = wall[h * chans + 2 * zz].astype(F32)
            two = wall[h * chans + 2 * zz + 1].astype(F32)
            at = 2 * short * h
            wpair[zz, at : at + short] = jnp.where(low, one, swap(two)).astype(BF16)
            wpair[zz, at + short : at + 2 * short] = jnp.where(low, swap(one), two).astype(BF16)

    total[...] = jnp.zeros_like(total)

    def gw_copy(dest, slot):
        return pltpu.make_async_remote_copy(
            src_ref=gw_out.at[dest], dst_ref=gw_in.at[slot], send_sem=gw_send.at[dest], recv_sem=gw_recv.at[slot],
            device_id=(dest, c), device_id_type=MESH,
        )

    def use(zz):
        pair = gathered[pl.ds(2 * zz, 2)].reshape(2 * width, blocks * rows)
        total[...] += jnp.dot(wpair[zz], pair, preferred_element_type=F32)
        product = lax.dot_general(feat_ref[...], pair, (((1,), (1,)), ((), ())), preferred_element_type=F32)
        for h in range(2):
            top = product[2 * short * h : 2 * short * h + short]
            low_part = product[2 * short * h + short : 2 * short * (h + 1)]
            pieces = (jnp.where(low, top, swap(low_part)), jnp.where(low, swap(top), low_part))
            for k in range(2):
                dest = h * chans + 2 * zz + k
                gw_out[dest] = pieces[k].astype(BF16)

                @pl.when(dest != n)
                def _():
                    gw_copy(dest, n).start()

                @pl.when(dest == n)
                def _():
                    gw_in[n] = pieces[k].astype(BF16)

    def sib_wait(t, zz):
        for q in range(chunks):
            sib_copy(t, zz, q).wait_recv()

    def finish(s):
        if s == 0:
            sib_wait(0, z)
            use(z)
        elif s < half:
            sib_wait(s, z)
            sib_wait(half + s, z)

            @pl.loop(0, 2)
            def _(side):
                use(lax.rem(z + side * s + (1 - side) * (depth - s), depth))
        else:
            sib_wait(half, z)
            use(lax.rem(z + half, depth))

    for s in range(1, half + 1):
        for q in range(chunks):
            if goes(s - 1, q, True):
                ring_copy(s - 1, q, True).wait_recv()
                send_on(s, q, True)
                sib_copy(s, lax.rem(z + depth - s, depth), q).start()
            if goes(s - 1, q, False):
                ring_copy(s - 1, q, False).wait_recv()
                send_on(s, q, False)
                sib_copy(half if s == half else half + s, lax.rem(z + s, depth), q).start()
        finish(s - 1)
    finish(half)
    gf_ref[...] = total[...].astype(BF16)

    @pl.loop(1, nodes)
    def _(r):
        gw_copy(peer(r), peer(nodes - r)).wait_recv()

    gw_sum[...] = jnp.sum(gw_in[...].astype(F32), axis=0)
    last = pltpu.make_async_remote_copy(
        src_ref=gw_sum, dst_ref=gw_last, send_sem=last_send, recv_sem=last_recv,
        device_id=(to_n, to_c), device_id_type=MESH,
    )

    @pl.when(to_self)
    def _():
        gw_ref[...] = gw_sum[...]

    @pl.when(jnp.logical_not(to_self))
    def _():
        last.start()
        last.wait()
        gw_ref[...] = gw_last[...]

    to_after.wait_send()
    to_before.wait_send()

    @pl.loop(1, nodes)
    def _(r):
        w_copy(r, n).wait_send()
        gw_copy(peer(r), n).wait_send()
        for q in range(chunks):
            un_copy(q, r, peer(r), n).wait_send()

    for q in range(chunks):
        for s in range(half):
            for to_right in (True, False):
                if goes(s, q, to_right):
                    ring_copy(s, q, to_right).wait_send()
        for t in range(2 * half):
            sib_copy(t, z, q).wait_send()


def local(
    features, weight, pre_clean, pre_corrupt, grad_clean, grad_corrupt, slopes, adj_vals, adj_cols, adj_count, shuffle_from
):
    nodes, chans = lax.axis_size("node"), lax.axis_size("chan")
    row_count, width = features.shape
    blocks, slots, rows, _ = adj_vals.shape
    reach = (slots - 1) // 2
    half = chans // 4
    chunks = 2
    n = lax.axis_index("node")
    vmem = pl.BlockSpec(memory_space=pltpu.VMEM)
    smem = pl.BlockSpec(memory_space=pltpu.SMEM)

    moved = lax.ppermute(
        weight,
        ("node", "chan"),
        [(a * chans + b, ((a % 2) * chans + b) * chans + a // 2) for a in range(nodes) for b in range(chans)],
    )
    short = weight.shape[0] // 2
    wpiece = jnp.concatenate([moved[:short], moved[short:]], axis=1)

    mine = lax.dynamic_slice_in_dim(shuffle_from, n * blocks, blocks)
    pick = jnp.sum(
        jnp.where((mine // blocks)[:, None] == jnp.arange(nodes)[None, :], jnp.arange(blocks)[:, None], 0), axis=0
    )
    my_blocks = n * blocks + jnp.arange(blocks)
    owner = jnp.arange(shuffle_from.shape[0]) // blocks
    come_from = jnp.sum(jnp.where(shuffle_from[None, :] == my_blocks[:, None], owner[None, :], 0), axis=1)

    slope = jnp.broadcast_to(slopes[:, None], (width, rows))
    main, before, after = pl.pallas_call(
        band_kernel,
        out_shape=(
            jax.ShapeDtypeStruct((blocks, 2 * width, rows), F32),
            jax.ShapeDtypeStruct((reach, 2 * width, rows), BF16),
            jax.ShapeDtypeStruct((reach, 2 * width, rows), BF16),
        ),
        in_specs=[smem, smem] + [vmem] * 6,
        out_specs=(vmem, vmem, vmem),
        scratch_shapes=[pltpu.VMEM((blocks + 2 * reach + 1, 2 * width, rows), F32)],
        compiler_params=pltpu.CompilerParams(vmem_limit_bytes=24 * 2**20),
        cost_estimate=pl.CostEstimate(flops=2 * blocks * slots * rows**3, bytes_accessed=5 * 2**20, transcendentals=0),
        name="band",
    )(adj_cols.T, adj_count, grad_clean.T, pre_clean.T, grad_corrupt.T, pre_corrupt.T, slope, adj_vals)

    part = width // chunks
    dma = pltpu.SemaphoreType.DMA
    gw, gf = pl.pallas_call(
        functools.partial(link_kernel, chunks),
        out_shape=(
            jax.ShapeDtypeStruct((short, 2 * width), F32),
            jax.ShapeDtypeStruct((width, row_count), BF16),
        ),
        in_specs=[smem, smem] + [vmem] * 5,
        out_specs=(vmem, vmem),
        scratch_shapes=[
            pltpu.VMEM((chans, width, row_count), BF16),
            pltpu.VMEM((blocks, width, rows), F32),
            pltpu.VMEM((blocks, width, rows), BF16),
            pltpu.VMEM((chunks, nodes, part, rows), BF16),
            pltpu.VMEM((nodes, part, rows), BF16),
            pltpu.VMEM((nodes, part, rows), BF16),
            pltpu.VMEM((2, reach, 2 * width, rows), BF16),
            pltpu.VMEM((nodes, short, 2 * width), BF16),
            pltpu.VMEM((chans // 2, 4 * short, 2 * width), BF16),
            pltpu.VMEM((width, row_count), F32),
            pltpu.VMEM((nodes, short, 2 * width), BF16),
            pltpu.VMEM((nodes, short, 2 * width), BF16),
            pltpu.VMEM((short, 2 * width), F32),
            pltpu.VMEM((short, 2 * width), F32),
            dma((2,)),
            dma((2,)),
            dma((nodes,)),
            dma((nodes,)),
            dma((chunks, nodes)),
            dma((chunks, nodes)),
            dma((half, chunks)),
            dma((half, chunks)),
            dma((half, chunks)),
            dma((half, chunks)),
            dma((2 * half, chunks)),
            dma((2 * half, chunks)),
            dma((nodes,)),
            dma((nodes,)),
            dma,
            dma,
        ],
        compiler_params=pltpu.CompilerParams(
            collective_id=0, has_side_effects=True, vmem_limit_bytes=32 * 2**20
        ),
        cost_estimate=pl.CostEstimate(
            flops=4 * row_count * width * width * chans, bytes_accessed=8 * 2**20, transcendentals=0
        ),
        name="link",
    )(pick, come_from, main, before, after, features.T, wpiece)
    grad_weight = jnp.concatenate([gw[:, :width], gw[:, width:]], axis=0)
    return (grad_weight, gf.T)


def solution(mesh):
    placed = (
        P("node", "chan"),
        P("node", "chan"),
        P("node", "chan"),
        P("node", "chan"),
        P("node", "chan"),
        P("node", "chan"),
        P("chan"),
        P("node", None, None, None),
        P("node", None),
        P("node"),
        P(),
    )
    return jax.shard_map(
        local,
        mesh=mesh,
        in_specs=placed,
        out_specs=(P("node", "chan"), P("node", "chan")),
        check_vma=False,
    )
```

time: 461 us -> 90.8 us (0.20)
  the two profiles are of different devices: /device:TPU:6 before, /device:TPU:4 now
where the time goes in v1:
time: 90.8 us; the launch traced here: 90.1 us
  Pallas kernels  67.9 us (75%)
  starting transfers between devices  10.9 us (12%)
  local copies, waits for them, and re-layouts  8.24 us (9%)
  other arithmetic  2.44 us (3%)
    pallas_call x1, Pallas kernels, local(): pl.pallas_call(functools.partial(link_kernel, chunks), out_shape=(jax.Sha...  66.3 us
    ppermute x1, starting transfers between devices, local(): lax.ppermute(weight, ('node', 'chan'), [(a * chans + b, (a % 2 * chans +...  10.9 us
    unnamed x17, local copies, waits for them, and re-layouts  7.43 us
  transfers between devices with their start and end apart: 1, of which 0 were waited for; matrix products, arithmetic and copies ran while one was open for 3% of the time, Pallas kernels for 2%

profile of v1, /device:TPU:4, one launch (start us, length us, event | category | flops | bytes accessed | tf_op | source)
XLA Modules:
  0.0 90.1 jit_solution(2506348346211909639)
XLA Ops:
  0.6 10.9 %collective-permute-start = (bf16[32,64]{1,0:T(8,128)(2,1)}, bf16[32,64]{1,0:T(8,128)(2,1)S(1)}, u32[]{:S(2)}, u32[]{:S(2)}) collective-permute-start(bf16[32,64]{1,0:T(8,128)(2,1)} %param.12), channel_id=1, source_target_pairs={{0,0},{1,16},{2,32},{3,48},{4,64},{5,80},{6,96},{7,112},{8,128},{9... | collective-permute-start | bytes 12296 | tf_op jit(solution)/shard_map/ppermute | solution.py:314
  11.5 0.8 and_select_fusion
  12.3 0.1 select_reduce_fusion.1.pick_ref
  12.4 0.9 select_reduce_fusion.from_ref
  13.3 0.7 broadcast_in_dim.40.slope_ref
  14.0 0.0 copy-start
  14.0 1.6 %copy-done = bf16[14,5,128,128]{3,2,1,0:T(8,128)(2,1)S(1)} copy-done((bf16[14,5,128,128]{3,2,1,0:T(8,128)(2,1)S(1)}, bf16[14,5,128,128]{3,2,1,0:T(8,128)(2,1)}, u32[]{:S(2)}) %copy-start) | copy-done | bytes 2293784
  15.6 0.0 copy-start.1
  15.6 0.9 %copy-done.1 = bf16[1792,64]{0,1:T(8,128)(2,1)S(1)} copy-done((bf16[1792,64]{0,1:T(8,128)(2,1)S(1)}, bf16[1792,64]{0,1:T(8,128)(2,1)}, u32[]{:S(2)}) %copy-start.1) | copy-done | bytes 229400
  16.6 0.0 copy-start.2
  16.6 0.9 %copy-done.2 = bf16[1792,64]{0,1:T(8,128)(2,1)S(1)} copy-done((bf16[1792,64]{0,1:T(8,128)(2,1)S(1)}, bf16[1792,64]{0,1:T(8,128)(2,1)}, u32[]{:S(2)}) %copy-start.2) | copy-done | bytes 229400
  17.5 0.0 copy-start.3
  17.5 0.9 %copy-done.3 = bf16[1792,64]{0,1:T(8,128)(2,1)S(1)} copy-done((bf16[1792,64]{0,1:T(8,128)(2,1)S(1)}, bf16[1792,64]{0,1:T(8,128)(2,1)}, u32[]{:S(2)}) %copy-start.3) | copy-done | bytes 229400
  18.5 0.9 %copy-done.4 = bf16[1792,64]{0,1:T(8,128)(2,1)S(1)} copy-done((bf16[1792,64]{0,1:T(8,128)(2,1)S(1)}, bf16[1792,64]{0,1:T(8,128)(2,1)}, u32[]{:S(2)}) %copy-start.4) | copy-done | bytes 229400
  19.4 0.7 copy-done.5
  20.1 0.7 copy-done.6
  20.7 1.5 %band.1 = (f32[14,128,128]{2,1,0:T(8,128)S(1)}, bf16[2,128,128]{2,1,0:T(8,128)(2,1)S(1)}, bf16[2,128,128]{2,1,0:T(8,128)(2,1)S(1)}) custom-call(s32[5,14]{1,0:T(8,128)S(1)} %bitcast.12, s32[14]{0:T(128)S(1)} %copy-done.6, bf16[64,1792]{1,0:T(8,128)(2,1)S(1)} %bitcast.8, bf16[64,1792]{1,0:T(8,128)(2,1)S(1)} %bitcast.9, bf16[64,1792]{1,0:T(8,128)(2,1)S(1)} %bitcast.10, ...), custom_call_target="tpu_custom_call" | custom-call | flops 293601280 | bytes 5242880 | tf_op jit(solution)/shard_map/band/pallas_call | solution.py:331
  22.3 0.0 collective-permute-done
  22.3 0.1 pad_maximum_fusion.1.wpiece_ref
  22.4 0.0 copy-done.7
  22.4 66.3 %link.1 = (f32[16,128]{1,0:T(8,128)S(1)}, bf16[64,1792]{1,0:T(8,128)(2,1)S(1)}) custom-call(s32[32]{0:T(128)S(1)} %select_reduce_fusion.1.pick_ref, s32[14]{0:T(128)S(1)} %select_reduce_fusion.from_ref, f32[14,128,128]{2,1,0:T(8,128)S(1)} %get-tuple-element.7.main_ref, bf16[2,128,128]{2,1,0:T(8,128)(2,1)S(1)} %get-tuple-element.8.before_ref, ...), custom_call_target="tpu_custom_call" | custom-call | flops 469762048 | bytes 8388608 | tf_op jit(solution)/shard_map/link/pallas_call | solution.py:348
  88.7 0.1 fusion.3
  88.8 0.6 pad_maximum_fusion
  89.4 0.7 copy.14
  (7 shorter events, 0.0 us)
Async XLA Ops:
  0.6 21.7 %collective-permute-start = (bf16[32,64]{1,0:T(8,128)(2,1)}, bf16[32,64]{1,0:T(8,128)(2,1)S(1)}, u32[]{:S(2)}, u32[]{:S(2)}) collective-permute-start(bf16[32,64]{1,0:T(8,128)(2,1)} %param.12), channel_id=1, source_target_pairs={{0,0},{1,16},{2,32},{3,48},{4,64},{5,80},{6,96},{7,112},{8,128},{9... | collective-permute-start | bytes 12296 | tf_op jit(solution)/shard_map/ppermute | solution.py:314
  14.0 1.7 %copy-start = (bf16[14,5,128,128]{3,2,1,0:T(8,128)(2,1)S(1)}, bf16[14,5,128,128]{3,2,1,0:T(8,128)(2,1)}, u32[]{:S(2)}) copy-start(bf16[14,5,128,128]{3,2,1,0:T(8,128)(2,1)} %adj_ref.1) | copy-start | bytes 6881284
  15.6 0.9 %copy-start.1 = (bf16[1792,64]{0,1:T(8,128)(2,1)S(1)}, bf16[1792,64]{0,1:T(8,128)(2,1)}, u32[]{:S(2)}) copy-start(bf16[1792,64]{0,1:T(8,128)(2,1)} %param.15) | copy-start | bytes 688132
  16.6 0.9 %copy-start.2 = (bf16[1792,64]{0,1:T(8,128)(2,1)S(1)}, bf16[1792,64]{0,1:T(8,128)(2,1)}, u32[]{:S(2)}) copy-start(bf16[1792,64]{0,1:T(8,128)(2,1)} %param.13) | copy-start | bytes 688132
  17.5 0.9 %copy-start.3 = (bf16[1792,64]{0,1:T(8,128)(2,1)S(1)}, bf16[1792,64]{0,1:T(8,128)(2,1)}, u32[]{:S(2)}) copy-start(bf16[1792,64]{0,1:T(8,128)(2,1)} %param.16) | copy-start | bytes 688132
  18.5 0.9 %copy-start.4 = (bf16[1792,64]{0,1:T(8,128)(2,1)S(1)}, bf16[1792,64]{0,1:T(8,128)(2,1)}, u32[]{:S(2)}) copy-start(bf16[1792,64]{0,1:T(8,128)(2,1)} %param.14) | copy-start | bytes 688132
  19.4 0.7 copy-start.5
  20.1 0.7 copy-start.6
  20.7 1.7 %copy-start.7 = (bf16[1792,64]{0,1:T(8,128)(2,1)S(1)}, bf16[1792,64]{0,1:T(8,128)(2,1)}, u32[]{:S(2)}) copy-start(bf16[1792,64]{0,1:T(8,128)(2,1)} %param.11) | copy-start | bytes 688132

commit v2 on v1

v2 whole, which is shorter than its diff:
```python
import functools

import jax
import jax.numpy as jnp
from jax import lax
from jax.experimental import pallas as pl
from jax.experimental.pallas import tpu as pltpu
from jax.sharding import PartitionSpec as P

MESH = pl.DeviceIdType.MESH
BF16 = jnp.bfloat16
F32 = jnp.float32


def band_kernel(
    cols_hbm, count_hbm, shuffle_hbm, gc_hbm, pc_hbm, gx_hbm, px_hbm, slope_hbm, adj_hbm,
    main_ref, before_ref, after_ref, pick_ref, from_ref,
    acc, row_vmem, adj_vmem, cols_ref, count_ref, shuffle_ref, slope_ref, row_sem, adj_sem, small_sem,
):
    blocks, slots, rows, _ = adj_vmem.shape
    nodes = pick_ref.shape[0]
    reach = (slots - 1) // 2
    me = lax.axis_index("node")
    base = me * blocks - reach
    row_copies = [
        pltpu.make_async_copy(hbm, row_vmem.at[i], row_sem.at[i]) for i, hbm in enumerate((gc_hbm, pc_hbm, gx_hbm, px_hbm))
    ]
    adj_copies = [pltpu.make_async_copy(adj_hbm.at[b], adj_vmem.at[b], adj_sem.at[b]) for b in range(blocks)]
    small = ((shuffle_hbm, shuffle_ref), (slope_hbm, slope_ref), (cols_hbm, cols_ref), (count_hbm, count_ref))
    small_copies = [pltpu.make_async_copy(src, dst, small_sem.at[i]) for i, (src, dst) in enumerate(small)]
    for copy in small_copies + row_copies + adj_copies:
        copy.start()
    acc[...] = jnp.zeros_like(acc)
    small_copies[0].wait()

    for d in range(nodes):
        pick_ref[d] = 0
    for i in range(blocks):
        pick_ref[shuffle_ref[me * blocks + i] // blocks] = i

    @pl.loop(0, nodes)
    def _(d):
        for i in range(blocks):
            at = shuffle_ref[d * blocks + i] - me * blocks
            from_ref[jnp.where(jnp.logical_and(at >= 0, at < blocks), at, blocks)] = d

    for copy in small_copies[1:]:
        copy.wait()
    slope = jnp.broadcast_to(slope_ref[...], (rows, slope_ref.shape[1])).T
    spare = blocks + 2 * reach
    for copy in row_copies:
        copy.wait()
    for b in range(blocks):
        here = slice(b * rows, (b + 1) * rows)

        def grad(g, p):
            g = row_vmem[g, :, here].astype(F32)
            return jnp.where(row_vmem[p, :, here].astype(F32) > 0, g, g * slope).astype(BF16)

        d = jnp.concatenate([grad(0, 1), grad(2, 3)], axis=0)
        adj_copies[b].wait()
        parts = [jnp.dot(d, adj_vmem[b, k], preferred_element_type=F32) for k in range(slots)]
        for k in range(slots):
            target = jnp.where(k < count_ref[b], cols_ref[k, b] - base, spare)
            acc[target] += parts[k]
    main_ref[...] = acc[reach : reach + blocks]
    before_ref[...] = acc[:reach].astype(BF16)
    after_ref[...] = acc[reach + blocks : spare].astype(BF16)


def link_kernel(
    chunks,
    pick_hbm, from_hbm, main_hbm, before_hbm, after_hbm, weight_hbm, feat_hbm,
    gw_ref, gf_ref,
    gathered, pick_ref, from_ref, main_ref, corrupt, outgoing, halo, wraw, wown, wgot, wall, wpair, feat, total, gw_out, gw_in, gw_sum, gw_last,
    halo_send, halo_recv, wone_send, wone_recv, w_send, w_recv, un_send, un_recv,
    cw_send, cw_recv, ccw_send, ccw_recv, sib_send, sib_recv, gw_send, gw_recv, last_send, last_recv, feat_sem, in_sem,
    *incoming,
):
    nodes = lax.axis_size("node")
    chans = lax.axis_size("chan")
    n = lax.axis_index("node")
    c = lax.axis_index("chan")
    depth = chans // 2
    half = depth // 2
    z = c // 2
    core = lax.rem(c, 2)
    blocks = main_ref.shape[0]
    width = feat.shape[0]
    rows = main_ref.shape[2]
    reach = before_hbm.shape[0]
    part = width // chunks
    short = wown.shape[0]
    right = 2 * lax.rem(z + 1, depth) + core
    left = 2 * lax.rem(z + depth - 1, depth) + core
    sib = 2 * z + 1 - core
    after = lax.rem(n + 1, nodes)
    before = lax.rem(n + nodes - 1, nodes)
    to_n, to_c = 2 * c + n // chans, lax.rem(n, chans)
    fr_n, fr_c = lax.rem(n, 2) * chans + c, n // 2
    to_self = jnp.logical_and(to_n == n, to_c == c)
    to_other = jnp.logical_not(to_self)

    def peer(r):
        return lax.rem(n + r, nodes)

    feat_copy = pltpu.make_async_copy(feat_hbm, feat, feat_sem)
    moves = ((main_hbm, main_ref), (pick_hbm, pick_ref), (from_hbm, from_ref), (weight_hbm, wraw))
    in_copies = [pltpu.make_async_copy(src, dst, in_sem.at[i]) for i, (src, dst) in enumerate(moves)]
    for copy in in_copies:
        copy.start()
    feat_copy.start()
    barrier = pltpu.get_barrier_semaphore()

    @pl.loop(1, nodes)
    def _(r):
        pl.semaphore_signal(barrier, inc=1, device_id=(peer(r), c), device_id_type=MESH)

    for who in (right, left, sib):
        pl.semaphore_signal(barrier, inc=1, device_id=(n, who), device_id_type=MESH)

    @pl.when(to_other)
    def _():
        pl.semaphore_signal(barrier, inc=1, device_id=(fr_n, fr_c), device_id_type=MESH)
        pl.semaphore_signal(barrier, inc=1, device_id=(to_n, to_c), device_id_type=MESH)

    total[...] = jnp.zeros_like(total)
    for copy in in_copies:
        copy.wait()
    for i in range(reach, blocks - reach):
        corrupt[i] = main_ref[i, width:].astype(BF16)
    wown[...] = jnp.concatenate([wraw[:short].astype(F32), wraw[short:].astype(F32)], axis=1).astype(BF16)

    @pl.when(to_other)
    def _():
        pl.semaphore_wait(barrier, nodes + 4)

    @pl.when(to_self)
    def _():
        pl.semaphore_wait(barrier, nodes + 2)

    def halo_copy(src, slot, side, to):
        return pltpu.make_async_remote_copy(
            src_ref=src.at[:, pl.ds(side * width, width)], dst_ref=halo.at[slot, side],
            send_sem=halo_send.at[slot, side], recv_sem=halo_recv.at[slot, side],
            device_id=(to, c), device_id_type=MESH,
        )

    halos = [[halo_copy(after_hbm, 0, side, after), halo_copy(before_hbm, 1, side, before)] for side in range(2)]
    for side in (1, 0):
        for copy in halos[side]:
            copy.start()

    w_one = pltpu.make_async_remote_copy(
        src_ref=wown, dst_ref=wgot, send_sem=wone_send, recv_sem=wone_recv,
        device_id=(fr_n, fr_c), device_id_type=MESH,
    )

    def w_copy(r, slot):
        return pltpu.make_async_remote_copy(
            src_ref=wgot, dst_ref=wall.at[slot], send_sem=w_send.at[r], recv_sem=w_recv.at[slot],
            device_id=(peer(r), c), device_id_type=MESH,
        )

    @pl.when(to_other)
    def _():
        w_one.start()

    @pl.when(to_self)
    def _():
        wgot[...] = wown[...]

    for copy in halos[1]:
        copy.wait_recv()
    for i in range(reach):
        corrupt[i] = (main_ref[i, width:] + halo[0, 1, i].astype(F32)).astype(BF16)
        j = blocks - reach + i
        corrupt[j] = (main_ref[j, width:] + halo[1, 1, i].astype(F32)).astype(BF16)

    def un_copy(q, r, dest, slot):
        return pltpu.make_async_remote_copy(
            src_ref=outgoing.at[dest, pl.ds(q * part, part)], dst_ref=incoming[q].at[slot],
            send_sem=un_send.at[q, r], recv_sem=un_recv.at[q, slot],
            device_id=(dest, c), device_id_type=MESH,
        )

    @pl.loop(1, nodes)
    def _(r):
        dest = peer(r)
        outgoing[dest] = corrupt[pick_ref[dest]]
        un_copy(0, r, dest, n).start()

    for q in range(1, chunks):

        @pl.loop(1, nodes)
        def _(r):
            un_copy(q, r, peer(r), n).start()

    for q in range(chunks):
        incoming[q][n] = corrupt[pick_ref[n], q * part : (q + 1) * part]

    @pl.when(to_other)
    def _():
        w_one.wait()

    @pl.loop(1, nodes)
    def _(r):
        w_copy(r, n).start()

    wall[n] = wgot[...]
    for copy in halos[0]:
        copy.wait_recv()

    def ring_copy(s, q, to_right):
        shard = 2 * lax.rem(z + (depth - s if to_right else s), depth) + core
        where = gathered.at[shard, pl.ds(q * part, part)]
        return pltpu.make_async_remote_copy(
            src_ref=where, dst_ref=where,
            send_sem=(cw_send if to_right else ccw_send).at[s, q],
            recv_sem=(cw_recv if to_right else ccw_recv).at[s, q],
            device_id=(n, right if to_right else left), device_id_type=MESH,
        )

    def sib_copy(t, zz, q):
        where = gathered.at[2 * zz + core, pl.ds(q * part, part)]
        return pltpu.make_async_remote_copy(
            src_ref=where, dst_ref=where, send_sem=sib_send.at[t, q], recv_sem=sib_recv.at[t, q],
            device_id=(n, sib), device_id_type=MESH,
        )

    def goes(s, q, to_right):
        return s + 1 < half or (s + 1 == half and (q < chunks // 2) == to_right)

    def send_on(s, q, to_right):
        if goes(s, q, to_right):
            ring_copy(s, q, to_right).start()

    def own(q):
        @pl.loop(1, nodes)
        def _(r):
            un_copy(q, r, peer(r), peer(nodes - r)).wait_recv()

        here = slice(q * part, (q + 1) * part)
        for i in range(blocks):
            block = main_ref[i, here] + incoming[q][from_ref[i]].astype(F32)
            if i < reach:
                block = block + halo[0, 0, i, here].astype(F32)
            if i >= blocks - reach:
                block = block + halo[1, 0, i - (blocks - reach), here].astype(F32)
            gathered[c, here, i * rows : (i + 1) * rows] = block.astype(BF16)
        send_on(0, q, True)
        send_on(0, q, False)
        sib_copy(0, z, q).start()

    def step(s, q):
        if goes(s - 1, q, True):
            ring_copy(s - 1, q, True).wait_recv()
            send_on(s, q, True)
            sib_copy(s, lax.rem(z + depth - s, depth), q).start()
        if goes(s - 1, q, False):
            ring_copy(s - 1, q, False).wait_recv()
            send_on(s, q, False)
            sib_copy(half if s == half else half + s, lax.rem(z + s, depth), q).start()

    low = lax.broadcasted_iota(jnp.int32, wown.shape, 1) < width

    def swap(value):
        return pltpu.roll(value, width, 1)

    def weights():
        @pl.loop(1, nodes)
        def _(r):
            w_copy(r, peer(nodes - r)).wait_recv()

        for zz in range(depth):
            for h in range(2):
                one = wall[h * chans + 2 * zz].astype(F32)
                two = wall[h * chans + 2 * zz + 1].astype(F32)
                at = 2 * short * h
                wpair[zz, at : at + short] = jnp.where(low, one, swap(two)).astype(BF16)
                wpair[zz, at + short : at + 2 * short] = jnp.where(low, swap(one), two).astype(BF16)

    def gw_copy(dest, slot):
        return pltpu.make_async_remote_copy(
            src_ref=gw_out.at[dest], dst_ref=gw_in.at[slot], send_sem=gw_send.at[dest], recv_sem=gw_recv.at[slot],
            device_id=(dest, c), device_id_type=MESH,
        )

    def use(zz):
        pair = gathered[pl.ds(2 * zz, 2)].reshape(2 * width, blocks * rows)
        product = lax.dot_general(feat[...], pair, (((1,), (1,)), ((), ())), preferred_element_type=F32)
        for h in range(2):
            top = product[2 * short * h : 2 * short * h + short]
            bottom = product[2 * short * h + short : 2 * short * (h + 1)]
            gw_out[h * chans + 2 * zz] = jnp.where(low, top, swap(bottom)).astype(BF16)
            gw_out[h * chans + 2 * zz + 1] = jnp.where(low, swap(top), bottom).astype(BF16)

    def finish(s):
        sides = (-s, s) if 0 < s < half else (s,)
        for side in sides:
            for q in range(chunks):
                sib_copy(half + s if 0 < side < half else s, z, q).wait_recv()
        count = 4 * len(sides)

        @pl.loop(0, len(sides))
        def _(i):
            use(lax.rem(z + depth - s + 2 * s * i, depth))

        @pl.loop(0, count)
        def _(i):
            j = lax.rem(i + n, count)
            zz = lax.rem(z + depth - s + 2 * s * (j // 4), depth)
            dest = (lax.rem(j, 4) // 2) * chans + 2 * zz + lax.rem(j, 2)

            @pl.when(dest != n)
            def _():
                gw_copy(dest, n).start()

            @pl.when(dest == n)
            def _():
                gw_in[n] = gw_out[n]

        @pl.loop(0, len(sides))
        def _(i):
            zz = lax.rem(z + depth - s + 2 * s * i, depth)
            pair = gathered[pl.ds(2 * zz, 2)].reshape(2 * width, blocks * rows)
            total[...] += jnp.dot(wpair[zz], pair, preferred_element_type=F32)

    for wave in range(half + chunks):
        if wave < chunks:
            own(wave)
        for s in range(half, 0, -1):
            if 0 <= wave - s < chunks:
                step(s, wave - s)
        if wave == chunks - 1:
            feat_copy.wait()
            weights()
        if wave >= chunks:
            finish(wave - chunks)
    finish(half)
    gf_ref[...] = total[...].astype(BF16)

    @pl.loop(1, nodes)
    def _(r):
        gw_copy(peer(r), peer(nodes - r)).wait_recv()

    gw_sum[...] = jnp.sum(gw_in[...].astype(F32), axis=0)
    last = pltpu.make_async_remote_copy(
        src_ref=gw_sum, dst_ref=gw_last, send_sem=last_send, recv_sem=last_recv,
        device_id=(to_n, to_c), device_id_type=MESH,
    )

    @pl.when(to_other)
    def _():
        last.start()

    for side in range(2):
        for copy in halos[side]:
            copy.wait_send()

    @pl.loop(1, nodes)
    def _(r):
        w_copy(r, n).wait_send()
        gw_copy(peer(r), n).wait_send()
        for q in range(chunks):
            un_copy(q, r, peer(r), n).wait_send()

    for q in range(chunks):
        for s in range(half):
            for to_right in (True, False):
                if goes(s, q, to_right):
                    ring_copy(s, q, to_right).wait_send()
        for t in range(2 * half):
            sib_copy(t, z, q).wait_send()

    @pl.when(to_self)
    def _():
        gw_ref[...] = gw_sum[...]

    @pl.when(to_other)
    def _():
        last.wait()
        gw_ref[...] = gw_last[...]


def local(
    features, weight, pre_clean, pre_corrupt, grad_clean, grad_corrupt, slopes, adj_vals, adj_cols, adj_count, shuffle_from
):
    nodes, chans = lax.axis_size("node"), lax.axis_size("chan")
    row_count, width = features.shape
    blocks, slots, rows, _ = adj_vals.shape
    reach = (slots - 1) // 2
    half = chans // 4
    chunks = 4
    short = weight.shape[0] // 2
    part = width // chunks
    vmem = pl.BlockSpec(memory_space=pltpu.VMEM)
    smem = pl.BlockSpec(memory_space=pltpu.SMEM)
    hbm = pl.BlockSpec(memory_space=pltpu.HBM)
    dma = pltpu.SemaphoreType.DMA

    main, before, after, pick, come_from = pl.pallas_call(
        band_kernel,
        out_shape=(
            jax.ShapeDtypeStruct((blocks, 2 * width, rows), F32),
            jax.ShapeDtypeStruct((reach, 2 * width, rows), BF16),
            jax.ShapeDtypeStruct((reach, 2 * width, rows), BF16),
            jax.ShapeDtypeStruct((nodes,), jnp.int32),
            jax.ShapeDtypeStruct((blocks + 2,), jnp.int32),
        ),
        in_specs=[hbm] * 9,
        out_specs=(vmem, vmem, vmem, smem, smem),
        scratch_shapes=[
            pltpu.VMEM((blocks + 2 * reach + 1, 2 * width, rows), F32),
            pltpu.VMEM((4, width, row_count), BF16),
            pltpu.VMEM((blocks, slots, rows, rows), BF16),
            pltpu.SMEM((slots, blocks), jnp.int32),
            pltpu.SMEM((blocks,), jnp.int32),
            pltpu.SMEM((nodes * blocks,), jnp.int32),
            pltpu.VMEM((1, width), F32),
            dma((4,)),
            dma((blocks,)),
            dma((4,)),
        ],
        compiler_params=pltpu.CompilerParams(vmem_limit_bytes=62 * 2**20),
        cost_estimate=pl.CostEstimate(flops=2 * blocks * slots * rows**3, bytes_accessed=5 * 2**20, transcendentals=0),
        name="band",
    )(
        adj_cols.T, adj_count, shuffle_from, grad_clean.T, pre_clean.T, grad_corrupt.T, pre_corrupt.T, slopes[None, :], adj_vals
    )

    gw, gf = pl.pallas_call(
        functools.partial(link_kernel, chunks),
        out_shape=(
            jax.ShapeDtypeStruct((short, 2 * width), F32),
            jax.ShapeDtypeStruct((width, row_count), BF16),
        ),
        in_specs=[hbm] * 7,
        out_specs=(vmem, vmem),
        scratch_shapes=[
            pltpu.VMEM((chans, width, row_count), BF16),
            pltpu.SMEM((nodes,), jnp.int32),
            pltpu.SMEM((blocks + 2,), jnp.int32),
            pltpu.VMEM((blocks, 2 * width, rows), F32),
            pltpu.VMEM((blocks, width, rows), BF16),
            pltpu.VMEM((nodes, width, rows), BF16),
            pltpu.VMEM((2, 2, reach, width, rows), BF16),
            pltpu.VMEM(weight.shape, BF16),
            pltpu.VMEM((short, 2 * width), BF16),
            pltpu.VMEM((short, 2 * width), BF16),
            pltpu.VMEM((nodes, short, 2 * width), BF16),
            pltpu.VMEM((chans // 2, 4 * short, 2 * width), BF16),
            pltpu.VMEM((width, row_count), BF16),
            pltpu.VMEM((width, row_count), F32),
            pltpu.VMEM((nodes, short, 2 * width), BF16),
            pltpu.VMEM((nodes, short, 2 * width), BF16),
            pltpu.VMEM((short, 2 * width), F32),
            pltpu.VMEM((short, 2 * width), F32),
            dma((2, 2)),
            dma((2, 2)),
            dma,
            dma,
            dma((nodes,)),
            dma((nodes,)),
            dma((chunks, nodes)),
            dma((chunks, nodes)),
            dma((half, chunks)),
            dma((half, chunks)),
            dma((half, chunks)),
            dma((half, chunks)),
            dma((2 * half, chunks)),
            dma((2 * half, chunks)),
            dma((nodes,)),
            dma((nodes,)),
            dma,
            dma,
            dma,
            dma((4,)),
        ]
        + [pltpu.VMEM((nodes, part, rows), BF16)] * chunks,
        compiler_params=pltpu.CompilerParams(
            collective_id=0, has_side_effects=True, vmem_limit_bytes=62 * 2**20
        ),
        cost_estimate=pl.CostEstimate(
            flops=4 * row_count * width * width * chans, bytes_accessed=8 * 2**20, transcendentals=0
        ),
        name="link",
    )(pick, come_from, main, before, after, weight, features.T)
    grad_weight = jnp.concatenate([gw[:, :width], gw[:, width:]], axis=0)
    return (grad_weight, gf.T)


def solution(mesh):
    placed = (
        P("node", "chan"),
        P("node", "chan"),
        P("node", "chan"),
        P("node", "chan"),
        P("node", "chan"),
        P("node", "chan"),
        P("chan"),
        P("node", None, None, None),
        P("node", None),
        P("node"),
        P(),
    )
    return jax.shard_map(
        local,
        mesh=mesh,
        in_specs=placed,
        out_specs=(P("node", "chan"), P("node", "chan")),
        check_vma=False,
    )
```

time: 90.8 us -> 86.4 us (0.952)
  Pallas kernels: 67.9 us -> 82.4 us
  starting transfers between devices: 10.9 us -> 0 us
  local copies, waits for them, and re-layouts: 8.24 us -> 2.49 us
  other arithmetic: 2.44 us -> 0.61 us
    ppermute x1 -> x0, starting transfers between devices: 10.9 us -> none  [local(): lax.ppermute(weight, ('node', 'chan'), [(a * chans + b, (a % 2 * chans +...]
    pallas_call x1, Pallas kernels: 66.3 us -> 76 us  [local(): pl.pallas_call(functools.partial(link_kernel, chunks), out_shape=(jax.Sha...]
    unnamed x17 -> x1, local copies, waits for them, and re-layouts: 7.43 us -> 1.64 us
    pallas_call x1, Pallas kernels: 1.54 us -> 6.4 us  [local(): pl.pallas_call(band_kernel, out_shape=(jax.ShapeDtypeStruct((blocks, 2 *...]
    reduce_sum x2 -> x0, other arithmetic: 0.95 us -> none  [the longest x1 0.86 us: local(): jnp.sum(jnp.where(shuffle_from[None, :] == my_blocks[:, None], owner[None...]
  transfers between devices with their start and end apart: 1 -> 0, of which waited for: 0 -> 0; matrix products, arithmetic and copies ran while one was open for 3% -> 0% of each run, Pallas kernels for 2% -> 0%
where the time goes in v2:
time: 86.4 us; the launch traced here: 86.1 us
  Pallas kernels  82.4 us (95%)
  local copies, waits for them, and re-layouts  2.49 us (3%)
    pallas_call x1, Pallas kernels, local(): pl.pallas_call(functools.partial(link_kernel, chunks), out_shape=(jax.Sha...  76 us
    pallas_call x1, Pallas kernels, local(): pl.pallas_call(band_kernel, out_shape=(jax.ShapeDtypeStruct((blocks, 2 *...  6.4 us

profile of v2, /device:TPU:4, one launch (start us, length us, event | category | flops | bytes accessed | tf_op | source)
XLA Modules:
  0.0 86.1 jit_solution(7492746893106551394)
XLA Ops:
  0.6 6.4 %band.1 = (f32[14,128,128]{2,1,0:T(8,128)}, bf16[2,128,128]{2,1,0:T(8,128)(2,1)}, bf16[2,128,128]{2,1,0:T(8,128)(2,1)}, s32[32]{0:T(128)}, s32[16]{0:T(128)}) custom-call(s32[5,14]{1,0:T(8,128)} %bitcast.13, s32[14]{0:T(128)} %count_hbm.1, s32[448]{0:T(512)} %shuffle_hbm.1, bf16[64,1792]{1,0:T(8,128)(2,1)} %bitcast.9, bf16[64,1792]{1,0:T(8,128)(2,1)} %bitcast.10, ...), custom_call_target="tpu_custom_call" | custom-call | flops 293601280 | bytes 5242880 | tf_op jit(solution)/shard_map/band/pallas_call | solution.py:402
  7.0 76.0 %link.1 = (f32[16,128]{1,0:T(8,128)}, bf16[64,1792]{1,0:T(8,128)(2,1)}) custom-call(s32[32]{0:T(128)} %get-tuple-element.9.pick_hbm, s32[16]{0:T(128)} %get-tuple-element.10.from_hbm, f32[14,128,128]{2,1,0:T(8,128)} %get-tuple-element.11.main_hbm, bf16[2,128,128]{2,1,0:T(8,128)(2,1)} %get-tuple-element.12.before_hbm, ...), custom_call_target="tpu_custom_call" | custom-call | flops 469762048 | bytes 8388608 | tf_op jit(solution)/shard_map/link/pallas_call | solution.py:432
  83.0 0.8 fusion
  83.9 0.6 pad_maximum_fusion
  84.5 1.6 %copy.14 = bf16[1792,64]{0,1:T(8,128)(2,1)} copy(bf16[1792,64]{0,1:T(8,128)(2,1)} %bitcast.8) | data formatting | bytes 458752

commit v3 on v2

--- a/solution.py
+++ b/solution.py
@@ -12,69 +12,15 @@
 F32 = jnp.float32
 
 
-def band_kernel(
-    cols_hbm, count_hbm, shuffle_hbm, gc_hbm, pc_hbm, gx_hbm, px_hbm, slope_hbm, adj_hbm,
-    main_ref, before_ref, after_ref, pick_ref, from_ref,
-    acc, row_vmem, adj_vmem, cols_ref, count_ref, shuffle_ref, slope_ref, row_sem, adj_sem, small_sem,
-):
-    blocks, slots, rows, _ = adj_vmem.shape
-    nodes = pick_ref.shape[0]
-    reach = (slots - 1) // 2
-    me = lax.axis_index("node")
-    base = me * blocks - reach
-    row_copies = [
-        pltpu.make_async_copy(hbm, row_vmem.at[i], row_sem.at[i]) for i, hbm in enumerate((gc_hbm, pc_hbm, gx_hbm, px_hbm))
-    ]
-    adj_copies = [pltpu.make_async_copy(adj_hbm.at[b], adj_vmem.at[b], adj_sem.at[b]) for b in range(blocks)]
-    small = ((shuffle_hbm, shuffle_ref), (slope_hbm, slope_ref), (cols_hbm, cols_ref), (count_hbm, count_ref))
-    small_copies = [pltpu.make_async_copy(src, dst, small_sem.at[i]) for i, (src, dst) in enumerate(small)]
-    for copy in small_copies + row_copies + adj_copies:
-        copy.start()
-    acc[...] = jnp.zeros_like(acc)
-    small_copies[0].wait()
-
-    for d in range(nodes):
-        pick_ref[d] = 0
-    for i in range(blocks):
-        pick_ref[shuffle_ref[me * blocks + i] // blocks] = i
-
-    @pl.loop(0, nodes)
-    def _(d):
-        for i in range(blocks):
-            at = shuffle_ref[d * blocks + i] - me * blocks
-            from_ref[jnp.where(jnp.logical_and(at >= 0, at < blocks), at, blocks)] = d
-
-    for copy in small_copies[1:]:
-        copy.wait()
-    slope = jnp.broadcast_to(slope_ref[...], (rows, slope_ref.shape[1])).T
-    spare = blocks + 2 * reach
-    for copy in row_copies:
-        copy.wait()
-    for b in range(blocks):
-        here = slice(b * rows, (b + 1) * rows)
-
-        def grad(g, p):
-            g = row_vmem[g, :, here].astype(F32)
-            return jnp.where(row_vmem[p, :, here].astype(F32) > 0, g, g * slope).astype(BF16)
-
-        d = jnp.concatenate([grad(0, 1), grad(2, 3)], axis=0)
-        adj_copies[b].wait()
-        parts = [jnp.dot(d, adj_vmem[b, k], preferred_element_type=F32) for k in range(slots)]
-        for k in range(slots):
-            target = jnp.where(k < count_ref[b], cols_ref[k, b] - base, spare)
-            acc[target] += parts[k]
-    main_ref[...] = acc[reach : reach + blocks]
-    before_ref[...] = acc[:reach].astype(BF16)
-    after_ref[...] = acc[reach + blocks : spare].astype(BF16)
-
-
-def link_kernel(
+def layer_kernel(
     chunks,
-    pick_hbm, from_hbm, main_hbm, before_hbm, after_hbm, weight_hbm, feat_hbm,
+    cols_hbm, count_hbm, shuffle_hbm, gc_hbm, pc_hbm, gx_hbm, px_hbm, slope_hbm, adj_hbm, weight_hbm, feat_hbm,
     gw_ref, gf_ref,
-    gathered, pick_ref, from_ref, main_ref, corrupt, outgoing, halo, wraw, wown, wgot, wall, wpair, feat, total, gw_out, gw_in, gw_sum, gw_last,
+    gathered, pick_ref, from_ref, cols_ref, count_ref, shuffle_ref, slope_ref, row_vmem, adj_vmem, acc,
+    edge, corrupt, outgoing, halo, wraw, wown, wgot, wall, wpair, feat, total, gw_out, gw_in, gw_sum, gw_last,
+    row_sem, adj_sem, small_sem,
     halo_send, halo_recv, wone_send, wone_recv, w_send, w_recv, un_send, un_recv,
-    cw_send, cw_recv, ccw_send, ccw_recv, sib_send, sib_recv, gw_send, gw_recv, last_send, last_recv, feat_sem, in_sem,
+    cw_send, cw_recv, ccw_send, ccw_recv, sib_send, sib_recv, gw_send, gw_recv, last_send, last_recv,
     *incoming,
 ):
     nodes = lax.axis_size("node")
@@ -85,10 +31,9 @@
     half = depth // 2
     z = c // 2
     core = lax.rem(c, 2)
-    blocks = main_ref.shape[0]
+    blocks, slots, rows, _ = adj_vmem.shape
     width = feat.shape[0]
-    rows = main_ref.shape[2]
-    reach = before_hbm.shape[0]
+    reach = (slots - 1) // 2
     part = width // chunks
     short = wown.shape[0]
     right = 2 * lax.rem(z + 1, depth) + core
@@ -96,20 +41,28 @@
     sib = 2 * z + 1 - core
     after = lax.rem(n + 1, nodes)
     before = lax.rem(n + nodes - 1, nodes)
-    to_n, to_c = 2 * c + n // chans, lax.rem(n, chans)
-    fr_n, fr_c = lax.rem(n, 2) * chans + c, n // 2
+    to_n, to_c = 2 * c + n // chans, 2 * lax.rem(n, depth) + lax.rem(n // depth, 2)
+    fr_n, fr_c = (2 * lax.rem(n, 2) + core) * depth + z, n // 2
     to_self = jnp.logical_and(to_n == n, to_c == c)
     to_other = jnp.logical_not(to_self)
 
     def peer(r):
         return lax.rem(n + r, nodes)
 
-    feat_copy = pltpu.make_async_copy(feat_hbm, feat, feat_sem)
-    moves = ((main_hbm, main_ref), (pick_hbm, pick_ref), (from_hbm, from_ref), (weight_hbm, wraw))
-    in_copies = [pltpu.make_async_copy(src, dst, in_sem.at[i]) for i, (src, dst) in enumerate(moves)]
-    for copy in in_copies:
+    edges = list(range(reach)) + list(range(blocks - reach, blocks))
+    order = edges + list(range(reach, blocks - reach))
+    row_copies = [
+        pltpu.make_async_copy(hbm, row_vmem.at[i], row_sem.at[i]) for i, hbm in enumerate((gc_hbm, pc_hbm, gx_hbm, px_hbm))
+    ]
+    adj_copies = [pltpu.make_async_copy(adj_hbm.at[b], adj_vmem.at[b], adj_sem.at[b]) for b in range(blocks)]
+    small = (
+        (cols_hbm, cols_ref), (count_hbm, count_ref), (slope_hbm, slope_ref), (shuffle_hbm, shuffle_ref),
+        (weight_hbm, wraw), (feat_hbm, feat),
+    )
+    small_copies = [pltpu.make_async_copy(src, dst, small_sem.at[i]) for i, (src, dst) in enumerate(small)]
+    for copy in small_copies[:3] + row_copies + [adj_copies[b] for b in order] + small_copies[3:]:
         copy.start()
-    feat_copy.start()
+
     barrier = pltpu.get_barrier_semaphore()
 
     @pl.loop(1, nodes)
@@ -124,11 +77,37 @@
         pl.semaphore_signal(barrier, inc=1, device_id=(fr_n, fr_c), device_id_type=MESH)
         pl.semaphore_signal(barrier, inc=1, device_id=(to_n, to_c), device_id_type=MESH)
 
-    total[...] = jnp.zeros_like(total)
-    for copy in in_copies:
+    base = n * blocks - reach
+    acc[...] = jnp.zeros_like(acc)
+    for copy in small_copies[:3]:
         copy.wait()
-    for i in range(reach, blocks - reach):
-        corrupt[i] = main_ref[i, width:].astype(BF16)
+    slope = jnp.broadcast_to(slope_ref[...], (rows, width)).T
+    for copy in row_copies:
+        copy.wait()
+
+    def band(b):
+        here = slice(b * rows, (b + 1) * rows)
+
+        def grad(g, p):
+            g = row_vmem[g, :, here].astype(F32)
+            return jnp.where(row_vmem[p, :, here].astype(F32) > 0, g, g * slope).astype(BF16)
+
+        d = jnp.concatenate([grad(0, 1), grad(2, 3)], axis=0)
+        adj_copies[b].wait()
+        parts = [jnp.dot(d, adj_vmem[b, k], preferred_element_type=F32) for k in range(slots)]
+        where = [jnp.where(k < count_ref[b], cols_ref[k, b] - base - b, -1) for k in range(slots)]
+        for o in range(slots):
+            value = parts[0] if o == reach else None
+            for k in range(1, slots):
+                term = jnp.where(where[k] == o, parts[k], 0.0)
+                value = term if value is None else value + term
+            acc[b + o] += value
+
+    for b in edges:
+        band(b)
+    edge[0] = acc[reach + blocks :].astype(BF16)
+    edge[1] = acc[:reach].astype(BF16)
+    small_copies[4].wait()
     wown[...] = jnp.concatenate([wraw[:short].astype(F32), wraw[short:].astype(F32)], axis=1).astype(BF16)
 
     @pl.when(to_other)
@@ -139,14 +118,14 @@
     def _():
         pl.semaphore_wait(barrier, nodes + 2)
 
-    def halo_copy(src, slot, side, to):
-        return pltpu.make_async_remote_copy(
-            src_ref=src.at[:, pl.ds(side * width, width)], dst_ref=halo.at[slot, side],
+    def halo_copy(slot, side, to):
+        return pltpu.make_async_remote_copy(
+            src_ref=edge.at[slot, :, pl.ds(side * width, width)], dst_ref=halo.at[slot, side],
             send_sem=halo_send.at[slot, side], recv_sem=halo_recv.at[slot, side],
             device_id=(to, c), device_id_type=MESH,
         )
 
-    halos = [[halo_copy(after_hbm, 0, side, after), halo_copy(before_hbm, 1, side, before)] for side in range(2)]
+    halos = [[halo_copy(0, side, after), halo_copy(1, side, before)] for side in range(2)]
     for side in (1, 0):
         for copy in halos[side]:
             copy.start()
@@ -170,12 +149,27 @@
     def _():
         wgot[...] = wown[...]
 
+    small_copies[3].wait()
+    taken = shuffle_ref[...]
+    at = lax.broadcasted_iota(jnp.int32, taken.shape, 1)
+    scale = (65536 + blocks - 1) // blocks
+    taken_node, at_node = (taken * scale) >> 16, (at * scale) >> 16
+    mine = at_node == n
+    for d in range(nodes):
+        pick_ref[d] = jnp.max(jnp.where(jnp.logical_and(mine, taken_node == d), at - n * blocks, 0))
+    for i in range(blocks):
+        from_ref[i] = jnp.max(jnp.where(taken == n * blocks + i, at_node, 0))
+
+    for b in range(reach, blocks - reach):
+        band(b)
+    for i in range(reach, blocks - reach):
+        corrupt[i] = acc[reach + i, width:].astype(BF16)
     for copy in halos[1]:
         copy.wait_recv()
     for i in range(reach):
-        corrupt[i] = (main_ref[i, width:] + halo[0, 1, i].astype(F32)).astype(BF16)
+        corrupt[i] = (acc[reach + i, width:] + halo[0, 1, i].astype(F32)).astype(BF16)
         j = blocks - reach + i
-        corrupt[j] = (main_ref[j, width:] + halo[1, 1, i].astype(F32)).astype(BF16)
+        corrupt[j] = (acc[reach + j, width:] + halo[1, 1, i].astype(F32)).astype(BF16)
 
     def un_copy(q, r, dest, slot):
         return pltpu.make_async_remote_copy(
@@ -242,7 +236,7 @@
 
         here = slice(q * part, (q + 1) * part)
         for i in range(blocks):
-            block = main_ref[i, here] + incoming[q][from_ref[i]].astype(F32)
+            block = acc[reach + i, here] + incoming[q][from_ref[i]].astype(F32)
             if i < reach:
                 block = block + halo[0, 0, i, here].astype(F32)
             if i >= blocks - reach:
@@ -274,8 +268,8 @@
 
         for zz in range(depth):
             for h in range(2):
-                one = wall[h * chans + 2 * zz].astype(F32)
-                two = wall[h * chans + 2 * zz + 1].astype(F32)
+                one = wall[2 * h * depth + zz].astype(F32)
+                two = wall[(2 * h + 1) * depth + zz].astype(F32)
                 at = 2 * short * h
                 wpair[zz, at : at + short] = jnp.where(low, one, swap(two)).astype(BF16)
                 wpair[zz, at + short : at + 2 * short] = jnp.where(low, swap(one), two).astype(BF16)
@@ -292,8 +286,8 @@
         for h in range(2):
             top = product[2 * short * h : 2 * short * h + short]
             bottom = product[2 * short * h + short : 2 * short * (h + 1)]
-            gw_out[h * chans + 2 * zz] = jnp.where(low, top, swap(bottom)).astype(BF16)
-            gw_out[h * chans + 2 * zz + 1] = jnp.where(low, swap(top), bottom).astype(BF16)
+            gw_out[2 * h * depth + zz] = jnp.where(low, top, swap(bottom)).astype(BF16)
+            gw_out[(2 * h + 1) * depth + zz] = jnp.where(low, swap(top), bottom).astype(BF16)
 
     def finish(s):
         sides = (-s, s) if 0 < s < half else (s,)
@@ -310,7 +304,7 @@
         def _(i):
             j = lax.rem(i + n, count)
             zz = lax.rem(z + depth - s + 2 * s * (j // 4), depth)
-            dest = (lax.rem(j, 4) // 2) * chans + 2 * zz + lax.rem(j, 2)
+            dest = lax.rem(j, 4) * depth + zz
 
             @pl.when(dest != n)
             def _():
@@ -324,19 +318,18 @@
         def _(i):
             zz = lax.rem(z + depth - s + 2 * s * i, depth)
             pair = gathered[pl.ds(2 * zz, 2)].reshape(2 * width, blocks * rows)
-            total[...] += jnp.dot(wpair[zz], pair, preferred_element_type=F32)
-
-    for wave in range(half + chunks):
-        if wave < chunks:
-            own(wave)
-        for s in range(half, 0, -1):
-            if 0 <= wave - s < chunks:
-                step(s, wave - s)
-        if wave == chunks - 1:
-            feat_copy.wait()
+            value = jnp.dot(wpair[zz], pair, preferred_element_type=F32)
+            total[...] = value if s == 0 else total[...] + value
+
+    for q in range(chunks):
+        own(q)
+    for s in range(1, half + 1):
+        for q in range(chunks):
+            step(s, q)
+        if s == 1:
+            small_copies[5].wait()
             weights()
-        if wave >= chunks:
-            finish(wave - chunks)
+        finish(s - 1)
     finish(half)
     gf_ref[...] = total[...].astype(BF16)
 
@@ -375,12 +368,14 @@
 
     @pl.when(to_self)
     def _():
-        gw_ref[...] = gw_sum[...]
+        gw_last[...] = gw_sum[...]
 
     @pl.when(to_other)
     def _():
         last.wait()
-        gw_ref[...] = gw_last[...]
+
+    gw_ref[:short] = gw_last[:, :width]
+    gw_ref[short:] = swap(gw_last[...])[:, :width]
 
 
 def local(
@@ -391,57 +386,32 @@
     blocks, slots, rows, _ = adj_vals.shape
     reach = (slots - 1) // 2
     half = chans // 4
-    chunks = 4
+    chunks = 2
     short = weight.shape[0] // 2
     part = width // chunks
     vmem = pl.BlockSpec(memory_space=pltpu.VMEM)
-    smem = pl.BlockSpec(memory_space=pltpu.SMEM)
     hbm = pl.BlockSpec(memory_space=pltpu.HBM)
     dma = pltpu.SemaphoreType.DMA
-
-    main, before, after, pick, come_from = pl.pallas_call(
-        band_kernel,
+    gw, gf = pl.pallas_call(
+        functools.partial(layer_kernel, chunks),
         out_shape=(
-            jax.ShapeDtypeStruct((blocks, 2 * width, rows), F32),
-            jax.ShapeDtypeStruct((reach, 2 * width, rows), BF16),
-            jax.ShapeDtypeStruct((reach, 2 * width, rows), BF16),
-            jax.ShapeDtypeStruct((nodes,), jnp.int32),
-            jax.ShapeDtypeStruct((blocks + 2,), jnp.int32),
-        ),
-        in_specs=[hbm] * 9,
-        out_specs=(vmem, vmem, vmem, smem, smem),
-        scratch_shapes=[
-            pltpu.VMEM((blocks + 2 * reach + 1, 2 * width, rows), F32),
-            pltpu.VMEM((4, width, row_count), BF16),
-            pltpu.VMEM((blocks, slots, rows, rows), BF16),
-            pltpu.SMEM((slots, blocks), jnp.int32),
-            pltpu.SMEM((blocks,), jnp.int32),
-            pltpu.SMEM((nodes * blocks,), jnp.int32),
-            pltpu.VMEM((1, width), F32),
-            dma((4,)),
-            dma((blocks,)),
-            dma((4,)),
-        ],
-        compiler_params=pltpu.CompilerParams(vmem_limit_bytes=62 * 2**20),
-        cost_estimate=pl.CostEstimate(flops=2 * blocks * slots * rows**3, bytes_accessed=5 * 2**20, transcendentals=0),
-        name="band",
-    )(
-        adj_cols.T, adj_count, shuffle_from, grad_clean.T, pre_clean.T, grad_corrupt.T, pre_corrupt.T, slopes[None, :], adj_vals
-    )
-
-    gw, gf = pl.pallas_call(
-        functools.partial(link_kernel, chunks),
-        out_shape=(
-            jax.ShapeDtypeStruct((short, 2 * width), F32),
+            jax.ShapeDtypeStruct((2 * short, width), F32),
             jax.ShapeDtypeStruct((width, row_count), BF16),
         ),
-        in_specs=[hbm] * 7,
+        in_specs=[hbm] * 11,
         out_specs=(vmem, vmem),
         scratch_shapes=[
             pltpu.VMEM((chans, width, row_count), BF16),
             pltpu.SMEM((nodes,), jnp.int32),
-            pltpu.SMEM((blocks + 2,), jnp.int32),
-            pltpu.VMEM((blocks, 2 * width, rows), F32),
+            pltpu.SMEM((blocks,), jnp.int32),
+            pltpu.SMEM((slots, blocks), jnp.int32),
+            pltpu.SMEM((blocks,), jnp.int32),
+            pltpu.VMEM((1, nodes * blocks), jnp.int32),
+            pltpu.VMEM((1, width), F32),
+            pltpu.VMEM((4, width, row_count), BF16),
+            pltpu.VMEM((blocks, slots, rows, rows), BF16),
+            pltpu.VMEM((blocks + 2 * reach, 2 * width, rows), F32),
+            pltpu.VMEM((2, reach, 2 * width, rows), BF16),
             pltpu.VMEM((blocks, width, rows), BF16),
             pltpu.VMEM((nodes, width, rows), BF16),
             pltpu.VMEM((2, 2, reach, width, rows), BF16),
@@ -456,6 +426,9 @@
             pltpu.VMEM((nodes, short, 2 * width), BF16),
             pltpu.VMEM((short, 2 * width), F32),
             pltpu.VMEM((short, 2 * width), F32),
+            dma((4,)),
+            dma((blocks,)),
+            dma((6,)),
             dma((2, 2)),
             dma((2, 2)),
             dma,
@@ -474,8 +447,6 @@
             dma((nodes,)),
             dma,
             dma,
-            dma,
-            dma((4,)),
         ]
         + [pltpu.VMEM((nodes, part, rows), BF16)] * chunks,
         compiler_params=pltpu.CompilerParams(
@@ -484,10 +455,12 @@
         cost_estimate=pl.CostEstimate(
             flops=4 * row_count * width * width * chans, bytes_accessed=8 * 2**20, transcendentals=0
         ),
-        name="link",
-    )(pick, come_from, main, before, after, weight, features.T)
-    grad_weight = jnp.concatenate([gw[:, :width], gw[:, width:]], axis=0)
-    return (grad_weight, gf.T)
+        name="layer",
+    )(
+        adj_cols.T, adj_count, shuffle_from[None, :], grad_clean.T, pre_clean.T, grad_corrupt.T, pre_corrupt.T,
+        slopes[None, :], adj_vals, weight, features.T,
+    )
+    return (gw, gf.T)
 
 
 def solution(mesh):

time: 86.4 us -> 74.1 us (0.86)
  Pallas kernels: 82.4 us -> 70.3 us
    pallas_call x2 -> x1, Pallas kernels: 82.4 us -> 70.3 us  [local(): pl.pallas_call(functools.partial(layer_kernel, chunks), out_shape=(jax.Sh...]
    unnamed x1 -> x2, local copies, waits for them, and re-layouts: 1.64 us -> 2.96 us
where the time goes in v3:
time: 74.1 us; the launch traced here: 73.9 us
  Pallas kernels  70.3 us (95%)
  local copies, waits for them, and re-layouts  2.96 us (4%)
    pallas_call x1, Pallas kernels, local(): pl.pallas_call(functools.partial(layer_kernel, chunks), out_shape=(jax.Sh...  70.3 us
    unnamed x2, local copies, waits for them, and re-layouts  2.96 us

profile of v3, /device:TPU:4, one launch (start us, length us, event | category | flops | bytes accessed | tf_op | source)
XLA Modules:
  0.0 73.9 jit_solution(5073597780771963511)
XLA Ops:
  0.6 70.3 %layer.1 = (f32[32,64]{1,0:T(8,128)}, bf16[64,1792]{1,0:T(8,128)(2,1)}) custom-call(s32[5,14]{1,0:T(8,128)} %bitcast.15, s32[14]{0:T(128)} %count_hbm.1, s32[1,448]{1,0:T(1,128)} %bitcast.16, bf16[64,1792]{1,0:T(8,128)(2,1)} %bitcast.9, bf16[64,1792]{1,0:T(8,128)(2,1)} %bitcast.10, bf16[64,1792]{1,0:T(8,128)(2,1)} %bitcast.11, bf16[64,1792]{1,0:T(8,128)(2,1)} %bitcast.12, ...), custom_call_target="tpu_custom_call" | custom-call | flops 469762048 | bytes 8388608 | tf_op jit(solution)/shard_map/layer/pallas_call | solution.py:395
  71.0 1.3 %copy.15 = f32[32,64]{1,0:T(8,128)} copy(f32[32,64]{1,0:T(8,128)} %get-tuple-element.8) | data formatting | bytes 16384
  72.3 1.6 %copy.16 = bf16[1792,64]{0,1:T(8,128)(2,1)} copy(bf16[1792,64]{0,1:T(8,128)(2,1)} %bitcast.14) | data formatting | bytes 458752

commit v4 on v3

--- a/solution.py
+++ b/solution.py
@@ -15,12 +15,12 @@
 def layer_kernel(
     chunks,
     cols_hbm, count_hbm, shuffle_hbm, gc_hbm, pc_hbm, gx_hbm, px_hbm, slope_hbm, adj_hbm, weight_hbm, feat_hbm,
-    gw_ref, gf_ref,
-    gathered, pick_ref, from_ref, cols_ref, count_ref, shuffle_ref, slope_ref, row_vmem, adj_vmem, acc,
-    edge, corrupt, outgoing, halo, wraw, wown, wgot, wall, wpair, feat, total, gw_out, gw_in, gw_sum, gw_last,
+    gw_ref, gf_hbm,
+    gathered, gf_ref, pick_ref, from_ref, cols_ref, count_ref, shuffle_ref, slope_ref, row_vmem, adj_vmem, acc,
+    edge, corrupt, outgoing, halo, wraw, wown, wgot, wall, wrows, feat, gw_out, gw_in, gw_sum, gw_last,
     row_sem, adj_sem, small_sem,
     halo_send, halo_recv, wone_send, wone_recv, w_send, w_recv, un_send, un_recv,
-    cw_send, cw_recv, ccw_send, ccw_recv, sib_send, sib_recv, gw_send, gw_recv, last_send, last_recv,
+    cw_send, cw_recv, ccw_send, ccw_recv, sib_send, sib_recv, gw_send, gw_recv, last_send, last_recv, gf_sem,
     *incoming,
 ):
     nodes = lax.axis_size("node")
@@ -49,6 +49,9 @@
     def peer(r):
         return lax.rem(n + r, nodes)
 
+    def turn(r):
+        return lax.rem(n + jnp.where(lax.rem(r, 2) == 1, (r + 1) // 2, nodes - r // 2), nodes)
+
     edges = list(range(reach)) + list(range(blocks - reach, blocks))
     order = edges + list(range(reach, blocks - reach))
     row_copies = [
@@ -138,7 +141,7 @@
     def w_copy(r, slot):
         return pltpu.make_async_remote_copy(
             src_ref=wgot, dst_ref=wall.at[slot], send_sem=w_send.at[r], recv_sem=w_recv.at[slot],
-            device_id=(peer(r), c), device_id_type=MESH,
+            device_id=(turn(r), c), device_id_type=MESH,
         )
 
     @pl.when(to_other)
@@ -180,7 +183,7 @@
 
     @pl.loop(1, nodes)
     def _(r):
-        dest = peer(r)
+        dest = turn(r)
         outgoing[dest] = corrupt[pick_ref[dest]]
         un_copy(0, r, dest, n).start()
 
@@ -188,20 +191,11 @@
 
         @pl.loop(1, nodes)
         def _(r):
-            un_copy(q, r, peer(r), n).start()
+            un_copy(q, r, turn(r), n).start()
 
     for q in range(chunks):
         incoming[q][n] = corrupt[pick_ref[n], q * part : (q + 1) * part]
 
-    @pl.when(to_other)
-    def _():
-        w_one.wait()
-
-    @pl.loop(1, nodes)
-    def _(r):
-        w_copy(r, n).start()
-
-    wall[n] = wgot[...]
     for copy in halos[0]:
         copy.wait_recv()
 
@@ -267,12 +261,13 @@
             w_copy(r, peer(nodes - r)).wait_recv()
 
         for zz in range(depth):
+            here = slice(2 * width * zz, 2 * width * (zz + 1))
             for h in range(2):
                 one = wall[2 * h * depth + zz].astype(F32)
                 two = wall[(2 * h + 1) * depth + zz].astype(F32)
                 at = 2 * short * h
-                wpair[zz, at : at + short] = jnp.where(low, one, swap(two)).astype(BF16)
-                wpair[zz, at + short : at + 2 * short] = jnp.where(low, swap(one), two).astype(BF16)
+                wrows[at : at + short, here] = jnp.where(low, one, swap(two)).astype(BF16)
+                wrows[at + short : at + 2 * short, here] = jnp.where(low, swap(one), two).astype(BF16)
 
     def gw_copy(dest, slot):
         return pltpu.make_async_remote_copy(
@@ -314,13 +309,6 @@
             def _():
                 gw_in[n] = gw_out[n]
 
-        @pl.loop(0, len(sides))
-        def _(i):
-            zz = lax.rem(z + depth - s + 2 * s * i, depth)
-            pair = gathered[pl.ds(2 * zz, 2)].reshape(2 * width, blocks * rows)
-            value = jnp.dot(wpair[zz], pair, preferred_element_type=F32)
-            total[...] = value if s == 0 else total[...] + value
-
     for q in range(chunks):
         own(q)
     for s in range(1, half + 1):
@@ -328,10 +316,33 @@
             step(s, q)
         if s == 1:
             small_copies[5].wait()
-            weights()
+
+            @pl.when(to_other)
+            def _():
+                w_one.wait()
+
+            wall[n] = wgot[...]
+        if s < half:
+
+            @pl.loop(1 + (nodes - 1) * (s - 1) // (half - 1), 1 + (nodes - 1) * s // (half - 1))
+            def _(r):
+                w_copy(r, n).start()
+
         finish(s - 1)
+    if half == 1:
+
+        @pl.loop(1, nodes)
+        def _(r):
+            w_copy(r, n).start()
+
     finish(half)
-    gf_ref[...] = total[...].astype(BF16)
+    weights()
+    tile = 2 * rows
+    for at in range(0, blocks * rows, tile):
+        sums = gathered[:, :, at : at + tile].reshape(chans * width, tile)
+        gf_ref[:, at : at + tile] = jnp.dot(wrows[...], sums, preferred_element_type=F32).astype(BF16)
+    gf_copy = pltpu.make_async_copy(gf_ref, gf_hbm, gf_sem)
+    gf_copy.start()
 
     @pl.loop(1, nodes)
     def _(r):
@@ -374,8 +385,10 @@
     def _():
         last.wait()
 
-    gw_ref[:short] = gw_last[:, :width]
-    gw_ref[short:] = swap(gw_last[...])[:, :width]
+    piece = gw_last[...]
+    gw_ref[:short] = piece[:, :width]
+    gw_ref[short:] = swap(piece)[:, :width]
+    gf_copy.wait()
 
 
 def local(
@@ -399,9 +412,10 @@
             jax.ShapeDtypeStruct((width, row_count), BF16),
         ),
         in_specs=[hbm] * 11,
-        out_specs=(vmem, vmem),
+        out_specs=(vmem, hbm),
         scratch_shapes=[
             pltpu.VMEM((chans, width, row_count), BF16),
+            pltpu.VMEM((width, row_count), BF16),
             pltpu.SMEM((nodes,), jnp.int32),
             pltpu.SMEM((blocks,), jnp.int32),
             pltpu.SMEM((slots, blocks), jnp.int32),
@@ -419,9 +433,8 @@
             pltpu.VMEM((short, 2 * width), BF16),
             pltpu.VMEM((short, 2 * width), BF16),
             pltpu.VMEM((nodes, short, 2 * width), BF16),
-            pltpu.VMEM((chans // 2, 4 * short, 2 * width), BF16),
+            pltpu.VMEM((4 * short, chans * width), BF16),
             pltpu.VMEM((width, row_count), BF16),
-            pltpu.VMEM((width, row_count), F32),
             pltpu.VMEM((nodes, short, 2 * width), BF16),
             pltpu.VMEM((nodes, short, 2 * width), BF16),
             pltpu.VMEM((short, 2 * width), F32),
@@ -447,6 +460,7 @@
             dma((nodes,)),
             dma,
             dma,
+            dma,
         ]
         + [pltpu.VMEM((nodes, part, rows), BF16)] * chunks,
         compiler_params=pltpu.CompilerParams(

time: 74.1 us -> 73 us (0.985)
  Pallas kernels: 70.3 us -> 69.2 us
    pallas_call x1, Pallas kernels: 70.3 us -> 69.2 us  [local(): pl.pallas_call(functools.partial(layer_kernel, chunks), out_shape=(jax.Sh...]
where the time goes in v4:
time: 73 us; the launch traced here: 72.8 us
  Pallas kernels  69.2 us (95%)
  local copies, waits for them, and re-layouts  2.96 us (4%)
    pallas_call x1, Pallas kernels, local(): pl.pallas_call(functools.partial(layer_kernel, chunks), out_shape=(jax.Sh...  69.2 us
    unnamed x2, local copies, waits for them, and re-layouts  2.96 us

profile of v4, /device:TPU:4, one launch (start us, length us, event | category | flops | bytes accessed | tf_op | source)
XLA Modules:
  0.0 72.8 jit_solution(6522530729290276962)
XLA Ops:
  0.6 69.2 %layer.1 = (f32[32,64]{1,0:T(8,128)}, bf16[64,1792]{1,0:T(8,128)(2,1)}) custom-call(s32[5,14]{1,0:T(8,128)} %bitcast.15, s32[14]{0:T(128)} %count_hbm.1, s32[1,448]{1,0:T(1,128)} %bitcast.16, bf16[64,1792]{1,0:T(8,128)(2,1)} %bitcast.9, bf16[64,1792]{1,0:T(8,128)(2,1)} %bitcast.10, bf16[64,1792]{1,0:T(8,128)(2,1)} %bitcast.11, bf16[64,1792]{1,0:T(8,128)(2,1)} %bitcast.12, ...), custom_call_target="tpu_custom_call" | custom-call | flops 469762048 | bytes 8388608 | tf_op jit(solution)/shard_map/layer/pallas_call | solution.py:408
  69.8 1.3 %copy.15 = f32[32,64]{1,0:T(8,128)} copy(f32[32,64]{1,0:T(8,128)} %get-tuple-element.8) | data formatting | bytes 16384
  71.2 1.6 %copy.16 = bf16[1792,64]{0,1:T(8,128)(2,1)} copy(bf16[1792,64]{0,1:T(8,128)(2,1)} %bitcast.14) | data formatting | bytes 458752

commit v5 on v4

--- a/solution.py
+++ b/solution.py
@@ -337,26 +337,27 @@
 
     finish(half)
     weights()
+
+    @pl.loop(1, nodes)
+    def _(r):
+        gw_copy(peer(r), peer(nodes - r)).wait_recv()
+
+    gw_sum[...] = jnp.sum(gw_in[...].astype(F32), axis=0)
+    last = pltpu.make_async_remote_copy(
+        src_ref=gw_sum, dst_ref=gw_last, send_sem=last_send, recv_sem=last_recv,
+        device_id=(to_n, to_c), device_id_type=MESH,
+    )
+
+    @pl.when(to_other)
+    def _():
+        last.start()
+
     tile = 2 * rows
     for at in range(0, blocks * rows, tile):
         sums = gathered[:, :, at : at + tile].reshape(chans * width, tile)
         gf_ref[:, at : at + tile] = jnp.dot(wrows[...], sums, preferred_element_type=F32).astype(BF16)
     gf_copy = pltpu.make_async_copy(gf_ref, gf_hbm, gf_sem)
     gf_copy.start()
-
-    @pl.loop(1, nodes)
-    def _(r):
-        gw_copy(peer(r), peer(nodes - r)).wait_recv()
-
-    gw_sum[...] = jnp.sum(gw_in[...].astype(F32), axis=0)
-    last = pltpu.make_async_remote_copy(
-        src_ref=gw_sum, dst_ref=gw_last, send_sem=last_send, recv_sem=last_recv,
-        device_id=(to_n, to_c), device_id_type=MESH,
-    )
-
-    @pl.when(to_other)
-    def _():
-        last.start()
 
     for side in range(2):
         for copy in halos[side]:

time: 73 us -> 73.1 us (level)
  no operation moved by 1% of the time
where the time goes in v5:
time: 73.1 us; the launch traced here: 72.9 us
  Pallas kernels  69.3 us (95%)
  local copies, waits for them, and re-layouts  2.96 us (4%)
    pallas_call x1, Pallas kernels, local(): pl.pallas_call(functools.partial(layer_kernel, chunks), out_shape=(jax.Sh...  69.3 us
    unnamed x2, local copies, waits for them, and re-layouts  2.96 us

profile of v5, /device:TPU:4, one launch (start us, length us, event | category | flops | bytes accessed | tf_op | source)
XLA Modules:
  0.0 72.9 jit_solution(10693472893641843584)
XLA Ops:
  0.6 69.3 %layer.1 = (f32[32,64]{1,0:T(8,128)}, bf16[64,1792]{1,0:T(8,128)(2,1)}) custom-call(s32[5,14]{1,0:T(8,128)} %bitcast.15, s32[14]{0:T(128)} %count_hbm.1, s32[1,448]{1,0:T(1,128)} %bitcast.16, bf16[64,1792]{1,0:T(8,128)(2,1)} %bitcast.9, bf16[64,1792]{1,0:T(8,128)(2,1)} %bitcast.10, bf16[64,1792]{1,0:T(8,128)(2,1)} %bitcast.11, bf16[64,1792]{1,0:T(8,128)(2,1)} %bitcast.12, ...), custom_call_target="tpu_custom_call" | custom-call | flops 469762048 | bytes 8388608 | tf_op jit(solution)/shard_map/layer/pallas_call | solution.py:409
  69.9 1.3 %copy.15 = f32[32,64]{1,0:T(8,128)} copy(f32[32,64]{1,0:T(8,128)} %get-tuple-element.8) | data formatting | bytes 16384
  71.2 1.6 %copy.16 = bf16[1792,64]{0,1:T(8,128)(2,1)} copy(bf16[1792,64]{0,1:T(8,128)(2,1)} %bitcast.14) | data formatting | bytes 458752
